TPU v7x, 32 devices: a whole 2x2x4 slice. The times are simulated.
32 devices in a mesh: wide: 8 (over z, x), narrow: 4 (over y, core).
Axes of the slice: x: 2, y: 2, z: 4, core: 2. Of those that a mesh axis runs over, the one named last changes fastest.
Arguments:
- latent: bfloat16 [8, 32, 48, 256], P('wide', 'narrow'), may hold values from -12 to 12
- conv_first: bfloat16 [6912, 256], P(None, 'wide'), may hold values from -0.078125 to 0.078125
- conv_second: bfloat16 [6912, 256], P(None, 'wide'), may hold values from -0.078125 to 0.078125
- embed_weight: bfloat16 [1024, 2240], P(None, 'wide'), may hold values from -0.1875 to 0.1875
- qkv_weight: bfloat16 [3, 2240, 2240], P(None, None, 'narrow'), may hold values from -0.125 to 0.125
Outputs:
- mixed: bfloat16 [3072, 2240], P('wide', 'narrow')
All inputs are finite; a program needn't handle non-finite values.
Results may differ from a plain program's by a relative error of at most 0.011.
Values may be sent and summed in bfloat16 or wider, within the bound.
A program may use at most 128 MiB of HBM per device.

v0:
```python
import jax
import jax.numpy as jnp
from jax import lax
from jax.sharding import PartitionSpec as P

HEAD_DIM = 112


def shifted(x, axis, by):
    size = lax.axis_size(axis)
    pairs = [(i, i + by) for i in range(size) if 0 <= i + by < size]
    return lax.ppermute(x, axis, pairs)


def extended(block, sides, width):
    for axis, dim in sides:
        count = lax.axis_size(axis)
        forward = [(i, i + 1) for i in range(count - 1)]
        backward = [(target, source) for source, target in forward]
        low = lax.ppermute(
            lax.slice_in_dim(block, block.shape[dim] - width, None, axis=dim), axis, forward
        )
        high = lax.ppermute(lax.slice_in_dim(block, 0, width, axis=dim), axis, backward)
        block = jnp.concatenate([low, block, high], axis=dim)
    return block


def causal_conv(current, weight):
    before = shifted(current, "wide", 1)
    earlier = shifted(current, "wide", 2)
    stacked = jnp.concatenate([earlier, before, current], axis=0)
    rimmed = extended(stacked, (("narrow", 1),), 1)
    padded = jnp.pad(rimmed, ((0, 0), (0, 0), (1, 1), (0, 0)))
    row_count = current.shape[1]
    col_count = current.shape[2]
    chan_count = current.shape[3]
    block_cols = lax.all_gather(weight, "wide", axis=1, tiled=True)
    summed = jnp.zeros((row_count * col_count, block_cols.shape[1]), jnp.float32)
    for kernel_tap in range(27):
        time_step = kernel_tap // 9
        row_step = kernel_tap // 3 % 3
        col_step = kernel_tap % 3
        window = padded[time_step, row_step : row_step + row_count, col_step : col_step + col_count]
        window = window.reshape(row_count * col_count, chan_count)
        summed = summed + jnp.dot(
            window,
            block_cols[kernel_tap * chan_count : (kernel_tap + 1) * chan_count],
            preferred_element_type=jnp.float32,
        )
    return summed


def embed_tokens(patch_feats, embed_weight):
    return jnp.dot(
        patch_feats,
        lax.all_gather(embed_weight, "wide", axis=1, tiled=True),
        preferred_element_type=jnp.float32,
    ).astype(jnp.bfloat16)


def per_device(latent, conv_first, conv_second, embed_weight, qkv_weight):
    row_count = latent.shape[1]
    col_count = latent.shape[2]
    chan_count = latent.shape[3]
    first = causal_conv(latent, conv_first)
    activated = jax.nn.silu(first).astype(jnp.bfloat16).reshape(latent.shape)
    second = causal_conv(activated, conv_second) + latent.reshape(-1, chan_count).astype(
        jnp.float32
    )
    block_out = second.astype(jnp.bfloat16)
    patches = block_out.reshape(row_count // 2, 2, col_count // 2, 2, chan_count)
    patches = patches.transpose(0, 2, 1, 3, 4).reshape(-1, 4 * chan_count)
    embedded = lax.all_gather(embed_tokens(patches, embed_weight), "narrow", axis=0, tiled=True)
    heads_here = qkv_weight.shape[2] // HEAD_DIM
    token_count = embedded.shape[0]
    query_raw = jnp.dot(embedded, qkv_weight[0], preferred_element_type=jnp.float32)
    key_raw = jnp.dot(embedded, qkv_weight[1], preferred_element_type=jnp.float32)
    val_rows = jnp.dot(embedded, qkv_weight[2], preferred_element_type=jnp.float32).astype(
        jnp.bfloat16
    )
    query_feat = (
        (jax.nn.elu(query_raw) + 1.0)
        .astype(jnp.bfloat16)
        .reshape(token_count, heads_here, HEAD_DIM)
    )
    key_feat = (
        (jax.nn.elu(key_raw) + 1.0).astype(jnp.bfloat16).reshape(token_count, heads_here, HEAD_DIM)
    )
    val_heads = val_rows.reshape(token_count, heads_here, HEAD_DIM)
    scores = jnp.einsum("thd,shd->hts", query_feat, key_feat, preferred_element_type=jnp.float32)
    row_ids = lax.broadcasted_iota(jnp.int32, (token_count, token_count), 0)
    col_ids = lax.broadcasted_iota(jnp.int32, (token_count, token_count), 1)
    scores = jnp.where((col_ids <= row_ids)[None], scores, 0.0)
    local_den = jnp.sum(scores, axis=-1)
    local_num = jnp.einsum(
        "hts,she->the", scores.astype(jnp.bfloat16), val_heads, preferred_element_type=jnp.float32
    )
    state_local = jnp.einsum(
        "thd,the->hde", key_feat, val_heads, preferred_element_type=jnp.float32
    )
    key_local = jnp.sum(key_feat, axis=0, dtype=jnp.float32)
    flat_state = jnp.concatenate([state_local.reshape(-1), key_local.reshape(-1)])
    length_all = flat_state.shape[0]
    peer_count = lax.axis_size("wide")
    per_peer = -(-length_all // peer_count)
    piece_grid = jnp.pad(flat_state, (0, per_peer * peer_count - length_all)).reshape(
        peer_count, per_peer
    )
    lower_ones = (
        lax.broadcasted_iota(jnp.int32, (peer_count, peer_count), 1)
        < lax.broadcasted_iota(jnp.int32, (peer_count, peer_count), 0)
    ).astype(jnp.float32)
    partial_sums = jnp.dot(
        lower_ones,
        lax.all_to_all(
            piece_grid.astype(jnp.bfloat16), "wide", split_axis=0, concat_axis=0, tiled=True
        ).astype(piece_grid.dtype),
        precision=lax.Precision.HIGHEST,
    )
    spread = lax.all_to_all(
        partial_sums.astype(jnp.bfloat16), "wide", split_axis=0, concat_axis=0, tiled=True
    ).astype(partial_sums.dtype)
    flat_prefix = spread.reshape(-1)[:length_all]
    state_size = state_local.size
    state_prev = flat_prefix[:state_size].reshape(state_local.shape)
    key_prev = flat_prefix[state_size:].reshape(key_local.shape)
    query_wide = query_feat.astype(jnp.float32)
    carried_num = jnp.einsum(
        "thd,hde->the", query_wide, state_prev, precision=lax.Precision.HIGHEST
    )
    carried_den = jnp.einsum("thd,hd->th", query_wide, key_prev, precision=lax.Precision.HIGHEST)
    result = (local_num + carried_num) / (local_den.T + carried_den)[..., None]
    return result.astype(jnp.bfloat16).reshape(token_count, heads_here * HEAD_DIM)


def solution(mesh):
    return jax.shard_map(
        per_device,
        mesh=mesh,
        in_specs=(
            P("wide", "narrow", None, None),
            P(None, "wide"),
            P(None, "wide"),
            P(None, "wide"),
            P(None, None, "narrow"),
        ),
        out_specs=P("wide", "narrow"),
        check_vma=False,
    )
```

profile of v0, /device:TPU:0, one launch (start us, length us, event | category | flops | bytes accessed | tf_op | source)
XLA Modules:
  0.0 299.9 jit_solution(16809636888822531081)
XLA Ops:
  8.1 4.9 %collective-permute-start = (bf16[1,8,48,256]{3,2,1,0:T(8,128)(2,1)}, bf16[1,8,48,256]{3,2,1,0:T(8,128)(2,1)S(1)}, u32[]{:S(2)}, u32[]{:S(2)}) collective-permute-start(bf16[1,8,48,256]{3,2,1,0:T(8,128)(2,1)} %param.5), channel_id=1, source_target_pairs={{0,8},{4,12},{8,16},{12,20},{16,24},{20,28},{1,9},{5,13},{9,17},{1... | collective-permute-start | bytes 589832 | tf_op jit(solution)/shard_map/ppermute | solution.py:12
  13.0 3.4 %collective-permute-start.1 = (bf16[1,8,48,256]{3,2,1,0:T(8,128)(2,1)}, bf16[1,8,48,256]{3,2,1,0:T(8,128)(2,1)S(1)}, u32[]{:S(2)}, u32[]{:S(2)}) collective-permute-start(bf16[1,8,48,256]{3,2,1,0:T(8,128)(2,1)} %param.5), channel_id=1, source_target_pairs={{0,4},{4,8},{8,12},{12,16},{16,20},{20,24},{24,28},{1,5},{5,9},{9,... | collective-permute-start | bytes 589832 | tf_op jit(solution)/shard_map/ppermute | solution.py:12
  17.5 3.1 %collective-permute-done.1 = bf16[1,8,48,256]{3,2,1,0:T(8,128)(2,1)S(1)} collective-permute-done((bf16[1,8,48,256]{3,2,1,0:T(8,128)(2,1)}, bf16[1,8,48,256]{3,2,1,0:T(8,128)(2,1)S(1)}, u32[]{:S(2)}, u32[]{:S(2)}) %collective-permute-start.1) | collective-permute-done | bytes 196640 | tf_op jit(solution)/shard_map/ppermute | solution.py:12
  21.7 1.3 collective-permute-start.2
  23.0 1.3 collective-permute-start.3
  24.4 3.5 %collective-permute-done.3 = bf16[3,1,48,256]{3,2,1,0:T(8,128)(2,1)S(1)} collective-permute-done((bf16[3,1,48,256]{3,2,1,0:T(8,128)(2,1)S(1)}, bf16[3,1,48,256]{3,2,1,0:T(8,128)(2,1)S(1)}, u32[]{:S(2)}, u32[]{:S(2)}) %collective-permute-start.3) | collective-permute-done | bytes 73760 | tf_op jit(solution)/shard_map/ppermute | solution.py:23
  29.0 1.2 fusion.142
  31.3 46.7 %all-gather.5.cloned.1.call-done = bf16[6912,256]{0,1:T(8,128)(2,1)} async-done(((bf16[6912,32]{0,1:T(8,128)(2,1)}), bf16[6912,256]{0,1:T(8,128)(2,1)}) %all-gather.5.cloned.1.call-update) | async-done | bytes 3538960 | tf_op jit(solution)/shard_map/all_gather | solution.py:37
  77.9 1.3 fusion.133
  79.2 1.2 fusion.127
  81.6 1.2 fusion.119
  89.6 3.2 %collective-permute-start.4 = (bf16[1,8,48,256]{3,2,1,0:T(8,128)(2,1)S(1)}, bf16[1,8,48,256]{3,2,1,0:T(8,128)(2,1)S(1)}, u32[]{:S(2)}, u32[]{:S(2)}) collective-permute-start(bf16[1,8,48,256]{3,2,1,0:T(8,128)(2,1)S(1)} %bitcast.173), channel_id=1, source_target_pairs={{0,8},{4,12},{8,16},{12,20},{16,24},{20,28},{1,9},{5,13},{9,17},{1... | collective-permute-start | bytes 589832 | tf_op jit(solution)/shard_map/ppermute | solution.py:12
  92.8 2.5 collective-permute-start.5
  95.3 6.1 %collective-permute-done.4 = bf16[1,8,48,256]{3,2,1,0:T(8,128)(2,1)S(1)} collective-permute-done((bf16[1,8,48,256]{3,2,1,0:T(8,128)(2,1)S(1)}, bf16[1,8,48,256]{3,2,1,0:T(8,128)(2,1)S(1)}, u32[]{:S(2)}, u32[]{:S(2)}) %collective-permute-start.4) | collective-permute-done | bytes 196640 | tf_op jit(solution)/shard_map/ppermute | solution.py:12
  101.5 1.3 collective-permute-start.7
  102.8 3.2 %collective-permute-start.6 = (bf16[3,1,48,256]{3,2,1,0:T(8,128)(2,1)S(1)}, bf16[3,1,48,256]{3,2,1,0:T(8,128)(2,1)S(1)}, u32[]{:S(2)}, u32[]{:S(2)}) collective-permute-start(bf16[3,1,48,256]{3,2,1,0:T(8,128)(2,1)S(1)} %get-tuple-element.53), channel_id=1, source_target_pairs={{0,1},{1,2},{2,3},{4,5},{5,6},{6,7},{8,9},{9,10},{10,11},{12,13},{... | collective-permute-start | bytes 221192 | tf_op jit(solution)/shard_map/ppermute | solution.py:20
  108.2 1.3 fusion.141
  109.5 41.4 %all-gather.7.cloned.1.call-done = bf16[6912,256]{0,1:T(8,128)(2,1)} async-done(((bf16[6912,32]{0,1:T(8,128)(2,1)}), bf16[6912,256]{0,1:T(8,128)(2,1)}) %all-gather.7.cloned.1.call-update) | async-done | bytes 3538960 | tf_op jit(solution)/shard_map/all_gather | solution.py:37
  150.9 1.3 fusion.98
  152.2 1.2 fusion.92
  162.9 67.1 %all-gather.9.cloned.1.call-done = bf16[1024,2240]{0,1:T(8,128)(2,1)} async-done(((bf16[1024,280]{0,1:T(8,128)(2,1)}), bf16[1024,2240]{0,1:T(8,128)(2,1)}) %all-gather.9.cloned.1.call-update) | async-done | bytes 4587536 | tf_op jit(solution)/shard_map/all_gather | solution.py:56
  229.9 4.6 %convolution_convert_fusion.1 = bf16[96,2240]{1,0:T(8,128)(2,1)} fusion(bf16[96,1024]{1,0:T(8,128)(2,1)S(1)} %reshape.66, bf16[1024,2240]{0,1:T(8,128)(2,1)} %all-gather.9.cloned.1.call-done), kind=kOutput, calls=%fused_computation.2 | convolution fusion | flops 440616960 | bytes 5214208 | tf_op jit(solution)/shard_map/dot_general | solution.py:54
  234.6 19.0 %all-gather.11.cloned.1.call-done = bf16[384,2240]{1,0:T(8,128)(2,1)} async-done(((bf16[96,2240]{1,0:T(8,128)(2,1)}), bf16[384,2240]{1,0:T(8,128)(2,1)}) %all-gather.11.cloned.1.call-update) | async-done | bytes 1720336 | tf_op jit(solution)/shard_map/all_gather | solution.py:73
  253.6 4.2 %fusion.144 = (bf16[560]{0:T(1024)(128)(2,1)S(1)}, bf16[384,560]{0,1:T(8,128)(2,1)S(1)}) fusion(bf16[384,2240]{1,0:T(8,128)(2,1)} %all-gather.11.cloned.1.call-done, bf16[3,2240,560]{1,2,0:T(8,128)(2,1)} %param.9), kind=kOutput, calls=%fused_computation.210 | convolution fusion | flops 964668864 | bytes 4781152 | tf_op jit(solution)/shard_map/dot_general | solution.py:77
  257.9 3.2 %fusion.17 = bf16[384,560]{0,1:T(8,128)(2,1)S(1)} fusion(bf16[384,2240]{1,0:T(8,128)(2,1)S(1)} %copy-done.30, bf16[3,2240,560]{1,2,0:T(8,128)(2,1)} %param.9), kind=kOutput, calls=%fused_computation.27 | convolution fusion | flops 963594240 | bytes 4730880 | tf_op jit(solution)/shard_map/dot_general | solution.py:78
  262.4 1.4 reduce.5
  264.6 5.5 %all-to-all-start = ((bf16[8,2,3955]{2,1,0:T(2,128)(2,1)}), bf16[8,2,3955]{2,1,0:T(2,128)(2,1)S(1)}, u32[]{:S(2)}, u32[]{:S(2)}) async-start(bf16[8,2,3955]{2,1,0:T(2,128)(2,1)} %reshape.78), calls=%async_computation | async-start | bytes 253952 | tf_op jit(solution)/shard_map/all_to_all | solution.py:115
  270.1 3.4 %fusion.43 = bf16[384,560]{0,1:T(8,128)(2,1)S(1)} fusion(bf16[384,2240]{1,0:T(8,128)(2,1)S(1)} %copy-done.30, bf16[3,2240,560]{1,2,0:T(8,128)(2,1)} %param.9), kind=kOutput, calls=%fused_computation.86 | convolution fusion | flops 964454400 | bytes 4730880 | tf_op jit(solution)/shard_map/dot_general | solution.py:76
  273.6 3.9 %all-to-all-done = bf16[8,2,3955]{2,1,0:T(2,128)(2,1)S(1)} async-done(((bf16[8,2,3955]{2,1,0:T(2,128)(2,1)}), bf16[8,2,3955]{2,1,0:T(2,128)(2,1)S(1)}, u32[]{:S(2)}, u32[]{:S(2)}) %all-to-all-start) | async-done | bytes 126592 | tf_op jit(solution)/shard_map/all_to_all | solution.py:115
  279.3 3.6 %all-to-all-start.1 = ((bf16[8,2,3955]{2,1,0:T(2,128)(2,1)}), bf16[8,2,3955]{2,1,0:T(2,128)(2,1)S(1)}, u32[]{:S(2)}, u32[]{:S(2)}) async-start(bf16[8,2,3955]{2,1,0:T(2,128)(2,1)} %reshape.80), calls=%async_computation.1 | async-start | bytes 253952 | tf_op jit(solution)/shard_map/all_to_all | solution.py:120
  283.5 6.3 %all-to-all-done.1 = bf16[8,2,3955]{2,1,0:T(2,128)(2,1)S(1)} async-done(((bf16[8,2,3955]{2,1,0:T(2,128)(2,1)}), bf16[8,2,3955]{2,1,0:T(2,128)(2,1)S(1)}, u32[]{:S(2)}, u32[]{:S(2)}) %all-to-all-start.1) | async-done | bytes 126592 | tf_op jit(solution)/shard_map/all_to_all | solution.py:120
  292.1 1.3 fusion.20
  (158 shorter events, 31.7 us)
Async XLA Ops:
  6.5 71.4 %all-gather.5.cloned.1.call-start = ((), (), s32[]{:S(2)}) async-start(), calls=%async_computation.2 | async-start | bytes 3981312 | tf_op jit(solution)/shard_map/all_gather | solution.py:37
  7.3 143.7 %all-gather.7.cloned.1.call-start = ((), (), s32[]{:S(2)}) async-start(), calls=%async_computation.3 | async-start | bytes 3981312 | tf_op jit(solution)/shard_map/all_gather | solution.py:37
  8.0 221.9 %all-gather.9.cloned.1.call-start = ((), (), s32[]{:S(2)}) async-start(), calls=%async_computation.4 | async-start | bytes 5160960 | tf_op jit(solution)/shard_map/all_gather | solution.py:56
  8.1 9.4 %collective-permute-start = (bf16[1,8,48,256]{3,2,1,0:T(8,128)(2,1)}, bf16[1,8,48,256]{3,2,1,0:T(8,128)(2,1)S(1)}, u32[]{:S(2)}, u32[]{:S(2)}) collective-permute-start(bf16[1,8,48,256]{3,2,1,0:T(8,128)(2,1)} %param.5), channel_id=1, source_target_pairs={{0,8},{4,12},{8,16},{12,20},{16,24},{20,28},{1,9},{5,13},{9,17},{1... | collective-permute-start | bytes 589832 | tf_op jit(solution)/shard_map/ppermute | solution.py:12
  13.0 7.6 %collective-permute-start.1 = (bf16[1,8,48,256]{3,2,1,0:T(8,128)(2,1)}, bf16[1,8,48,256]{3,2,1,0:T(8,128)(2,1)S(1)}, u32[]{:S(2)}, u32[]{:S(2)}) collective-permute-start(bf16[1,8,48,256]{3,2,1,0:T(8,128)(2,1)} %param.5), channel_id=1, source_target_pairs={{0,4},{4,8},{8,12},{12,16},{16,20},{20,24},{24,28},{1,5},{5,9},{9,... | collective-permute-start | bytes 589832 | tf_op jit(solution)/shard_map/ppermute | solution.py:12
  17.4 4.2 %copy-start.23 = (bf16[1,8,48,256]{3,2,1,0:T(8,128)(2,1)}, bf16[1,8,48,256]{3,2,1,0:T(8,128)(2,1)S(1)}, u32[]{:S(2)}) copy-start(bf16[1,8,48,256]{3,2,1,0:T(8,128)(2,1)S(1)} %collective-permute-done) | copy-start | bytes 589828
  21.7 2.7 collective-permute-start.2
  23.0 4.9 %collective-permute-start.3 = (bf16[3,1,48,256]{3,2,1,0:T(8,128)(2,1)S(1)}, bf16[3,1,48,256]{3,2,1,0:T(8,128)(2,1)S(1)}, u32[]{:S(2)}, u32[]{:S(2)}) collective-permute-start(bf16[3,1,48,256]{3,2,1,0:T(8,128)(2,1)S(1)} %get-tuple-element.59), channel_id=1, source_target_pairs={{1,0},{2,1},{3,2},{5,4},{6,5},{7,6},{9,8},{10,9},{11,10},{13,12},{... | collective-permute-start | bytes 221192 | tf_op jit(solution)/shard_map/ppermute | solution.py:23
  24.3 229.3 %all-gather.11.cloned.1.call-start = ((), (), s32[]{:S(2)}) async-start(), calls=%async_computation.5 | async-start | bytes 2211840 | tf_op jit(solution)/shard_map/all_gather | solution.py:73
  24.4 3.5 %copy-start.25 = (bf16[3,1,48,256]{3,2,1,0:T(8,128)(2,1)}, bf16[3,1,48,256]{3,2,1,0:T(8,128)(2,1)S(1)}, u32[]{:S(2)}) copy-start(bf16[3,1,48,256]{3,2,1,0:T(8,128)(2,1)S(1)} %collective-permute-done.2) | copy-start | bytes 221188
  77.9 6.0 %copy-start.1 = (bf16[6912,256]{0,1:T(8,128)(2,1)S(1)}, bf16[6912,256]{0,1:T(8,128)(2,1)}, u32[]{:S(2)}) copy-start(bf16[6912,256]{0,1:T(8,128)(2,1)} %all-gather.5.cloned.1.call-done) | copy-start | bytes 10616836
  77.9 6.7 %copy-start.20 = (bf16[1,8,48,256]{3,2,1,0:T(8,128)(2,1)S(1)}, bf16[1,8,48,256]{3,2,1,0:T(8,128)(2,1)}, u32[]{:S(2)}) copy-start(bf16[1,8,48,256]{3,2,1,0:T(8,128)(2,1)} %get-tuple-element.55) | copy-start | bytes 589828
  77.9 7.0 %copy-start.6 = (bf16[1,8,48,256]{3,2,1,0:T(8,128)(2,1)S(1)}, bf16[1,8,48,256]{3,2,1,0:T(8,128)(2,1)}, u32[]{:S(2)}) copy-start(bf16[1,8,48,256]{3,2,1,0:T(8,128)(2,1)} %get-tuple-element.38) | copy-start | bytes 589828
  79.2 6.0 %copy-start.5 = (bf16[1,8,48,256]{3,2,1,0:T(8,128)(2,1)S(1)}, bf16[1,8,48,256]{3,2,1,0:T(8,128)(2,1)}, u32[]{:S(2)}) copy-start(bf16[1,8,48,256]{3,2,1,0:T(8,128)(2,1)} %get-tuple-element.37) | copy-start | bytes 589828
  81.6 3.9 %copy-start.24 = (bf16[1,8,48,256]{3,2,1,0:T(8,128)(2,1)S(1)}, bf16[1,8,48,256]{3,2,1,0:T(8,128)(2,1)}, u32[]{:S(2)}) copy-start(bf16[1,8,48,256]{3,2,1,0:T(8,128)(2,1)} %copy-done.23) | copy-start | bytes 589828
  83.9 1.8 copy-start.3
  84.2 1.8 copy-start.19
  84.9 1.6 copy-start.17
  89.6 11.8 %collective-permute-start.4 = (bf16[1,8,48,256]{3,2,1,0:T(8,128)(2,1)S(1)}, bf16[1,8,48,256]{3,2,1,0:T(8,128)(2,1)S(1)}, u32[]{:S(2)}, u32[]{:S(2)}) collective-permute-start(bf16[1,8,48,256]{3,2,1,0:T(8,128)(2,1)S(1)} %bitcast.173), channel_id=1, source_target_pairs={{0,8},{4,12},{8,16},{12,20},{16,24},{20,28},{1,9},{5,13},{9,17},{1... | collective-permute-start | bytes 589832 | tf_op jit(solution)/shard_map/ppermute | solution.py:12
  92.8 8.6 %collective-permute-start.5 = (bf16[1,8,48,256]{3,2,1,0:T(8,128)(2,1)S(1)}, bf16[1,8,48,256]{3,2,1,0:T(8,128)(2,1)S(1)}, u32[]{:S(2)}, u32[]{:S(2)}) collective-permute-start(bf16[1,8,48,256]{3,2,1,0:T(8,128)(2,1)S(1)} %bitcast.174), channel_id=1, source_target_pairs={{0,4},{4,8},{8,12},{12,16},{16,20},{20,24},{24,28},{1,5},{5,9},{9,... | collective-permute-start | bytes 589832 | tf_op jit(solution)/shard_map/ppermute | solution.py:12
  101.5 4.5 %collective-permute-start.7 = (bf16[3,1,48,256]{3,2,1,0:T(8,128)(2,1)S(1)}, bf16[3,1,48,256]{3,2,1,0:T(8,128)(2,1)S(1)}, u32[]{:S(2)}, u32[]{:S(2)}) collective-permute-start(bf16[3,1,48,256]{3,2,1,0:T(8,128)(2,1)S(1)} %get-tuple-element.54), channel_id=1, source_target_pairs={{1,0},{2,1},{3,2},{5,4},{6,5},{7,6},{9,8},{10,9},{11,10},{13,12},{... | collective-permute-start | bytes 221192 | tf_op jit(solution)/shard_map/ppermute | solution.py:23
  102.8 4.1 %collective-permute-start.6 = (bf16[3,1,48,256]{3,2,1,0:T(8,128)(2,1)S(1)}, bf16[3,1,48,256]{3,2,1,0:T(8,128)(2,1)S(1)}, u32[]{:S(2)}, u32[]{:S(2)}) collective-permute-start(bf16[3,1,48,256]{3,2,1,0:T(8,128)(2,1)S(1)} %get-tuple-element.53), channel_id=1, source_target_pairs={{0,1},{1,2},{2,3},{4,5},{5,6},{6,7},{8,9},{9,10},{10,11},{12,13},{... | collective-permute-start | bytes 221192 | tf_op jit(solution)/shard_map/ppermute | solution.py:20
  150.9 6.0 %copy-start = (bf16[6912,256]{0,1:T(8,128)(2,1)S(1)}, bf16[6912,256]{0,1:T(8,128)(2,1)}, u32[]{:S(2)}) copy-start(bf16[6912,256]{0,1:T(8,128)(2,1)} %all-gather.7.cloned.1.call-done) | copy-start | bytes 10616836
  150.9 6.7 %copy-start.18 = (bf16[1,8,48,256]{3,2,1,0:T(8,128)(2,1)S(1)}, bf16[1,8,48,256]{3,2,1,0:T(8,128)(2,1)}, u32[]{:S(2)}) copy-start(bf16[1,8,48,256]{3,2,1,0:T(8,128)(2,1)} %get-tuple-element.45) | copy-start | bytes 589828
  150.9 7.0 %copy-start.9 = (bf16[1,8,48,256]{3,2,1,0:T(8,128)(2,1)S(1)}, bf16[1,8,48,256]{3,2,1,0:T(8,128)(2,1)}, u32[]{:S(2)}) copy-start(bf16[1,8,48,256]{3,2,1,0:T(8,128)(2,1)} %get-tuple-element.20) | copy-start | bytes 589828
  152.2 5.9 %copy-start.8 = (bf16[1,8,48,256]{3,2,1,0:T(8,128)(2,1)S(1)}, bf16[1,8,48,256]{3,2,1,0:T(8,128)(2,1)}, u32[]{:S(2)}) copy-start(bf16[1,8,48,256]{3,2,1,0:T(8,128)(2,1)} %get-tuple-element.19) | copy-start | bytes 589828
  156.9 1.8 copy-start.7
  157.1 1.8 copy-start.13
  157.6 1.6 copy-start.4
  253.6 4.3 %copy-start.30 = (bf16[384,2240]{1,0:T(8,128)(2,1)S(1)}, bf16[384,2240]{1,0:T(8,128)(2,1)}, u32[]{:S(2)}) copy-start(bf16[384,2240]{1,0:T(8,128)(2,1)} %all-gather.11.cloned.1.call-done) | copy-start | bytes 5160964
  264.6 12.8 %all-to-all-start = ((bf16[8,2,3955]{2,1,0:T(2,128)(2,1)}), bf16[8,2,3955]{2,1,0:T(2,128)(2,1)S(1)}, u32[]{:S(2)}, u32[]{:S(2)}) async-start(bf16[8,2,3955]{2,1,0:T(2,128)(2,1)} %reshape.78), calls=%async_computation | async-start | bytes 253952 | tf_op jit(solution)/shard_map/all_to_all | solution.py:115
  279.3 10.6 %all-to-all-start.1 = ((bf16[8,2,3955]{2,1,0:T(2,128)(2,1)}), bf16[8,2,3955]{2,1,0:T(2,128)(2,1)S(1)}, u32[]{:S(2)}, u32[]{:S(2)}) async-start(bf16[8,2,3955]{2,1,0:T(2,128)(2,1)} %reshape.80), calls=%async_computation.1 | async-start | bytes 253952 | tf_op jit(solution)/shard_map/all_to_all | solution.py:120
  (13 other events, 16.5 us)
Sparse Core Ops, SparseCore 0:
  9.5 68.3 all-gather.4
  80.1 70.7 all-gather.6
  153.1 76.7 all-gather.8
  234.7 18.8 all-gather.10
where the time goes:
time: 301 us; the launch traced here: 300 us
  waiting for transfers between devices  200 us (66%)
  matrix products  41 us (14%)
  starting transfers between devices  30.3 us (10%)
  between operations  14 us (5%)
  local copies, waits for them, and re-layouts  8.34 us (3%)
  other arithmetic  6.58 us (2%)
    all_gather x2, waiting for transfers between devices, causal_conv(): block_cols = lax.all_gather(weight, 'wide', axis=1, tiled=True)  88.1 us
    all_gather x1, waiting for transfers between devices, embed_tokens(): lax.all_gather(embed_weight, 'wide', axis=1, tiled=True)  67.1 us
    dot_general x54, matrix products, causal_conv(): jnp.dot(window, block_cols[kernel_tap * chan_count:(kernel_tap + 1) * cha...  22.6 us
    all_gather x1, waiting for transfers between devices, per_device(): lax.all_gather(embed_tokens(patches, embed_weight), 'narrow', axis=0, til...  19 us
    ppermute x4, starting transfers between devices, shifted(): return lax.ppermute(x, axis, pairs)  14 us
    ppermute x4, waiting for transfers between devices, shifted(): return lax.ppermute(x, axis, pairs)  10.3 us
    all_to_all x1, waiting for transfers between devices, per_device(): lax.all_to_all(partial_sums.astype(jnp.bfloat16), 'wide', split_axis=0, c...  6.35 us
  transfers between devices with their start and end apart: 14, of which 10 were waited for; matrix products, arithmetic and copies ran while one was open for 11% of the time, Pallas kernels for 0%

commit v1 on v0

--- a/solution.py
+++ b/solution.py
@@ -1,9 +1,219 @@
+import functools
+
 import jax
 import jax.numpy as jnp
 from jax import lax
+from jax.experimental import pallas as pl
+from jax.experimental.pallas import tpu as pltpu
 from jax.sharding import PartitionSpec as P
 
 HEAD_DIM = 112
+LANE = 128
+MESH = pl.DeviceIdType.MESH
+
+
+def strips(lanes):
+    half = lanes // LANE // 2
+    return half, max(1, half // 3)
+
+
+def gather_kernel(wide, narrow, shapes, *refs):
+    count = len(shapes)
+    mine, full = refs[:count], refs[count : 2 * count]
+    own_sem, send_sem, recv_sem = refs[2 * count :]
+    w = lax.axis_index("wide")
+    n = lax.axis_index("narrow")
+    z, x = w // 2, lax.rem(w, 2)
+    y, core = lax.rem(n // 2, 2), lax.rem(n, 2)
+    depth = wide // 2
+    peer_x = {"wide": w + 1 - 2 * x}
+    peer_y = {"narrow": n + 2 - 4 * y}
+    peer_core = {"narrow": n + 1 - 2 * core}
+    above, below = {"wide": w + 2}, {"wide": w - 2}
+    has_above, has_below = z < depth - 1, z > 0
+
+    barrier = pltpu.get_barrier_semaphore()
+    for peer in (peer_x, peer_y, peer_core):
+        pl.semaphore_signal(barrier, inc=1, device_id=peer, device_id_type=MESH)
+
+    @pl.when(has_above)
+    def _():
+        pl.semaphore_signal(barrier, inc=1, device_id=above, device_id_type=MESH)
+
+    @pl.when(has_below)
+    def _():
+        pl.semaphore_signal(barrier, inc=1, device_id=below, device_id_type=MESH)
+
+    pl.semaphore_wait(barrier, 3 + has_above.astype(jnp.int32) + has_below.astype(jnp.int32))
+
+    def window(part, shard, kind):
+        half, third = strips(shapes[part][1])
+        start, size = {
+            "own": (core * half + y * third, half - third),
+            "to_y": (core * half + y * (half - third), third),
+            "from_y": (core * half + (1 - y) * (half - third), third),
+            "core_own": ((1 - core) * half + y * third, half - third),
+            "core_y": ((1 - core) * half + (1 - y) * (half - third), third),
+        }[kind]
+        cols = pl.ds(pl.multiple_of(start * LANE, LANE), size * LANE)
+        return (shard, slice(None), cols)
+
+    def transfer(part, shard, kind, lane, peer, own=False):
+        at = window(part, shard, kind)
+        target = full[part].at[at]
+        source = mine[part].at[at[1:]] if own else target
+        arrive = {"own": 0, "to_y": 1, "from_y": 3}[kind]
+        if lane == "core" and kind == "own":
+            arrive = 2
+        send = ("up", "down", "x", "y", "core", "core_y").index(lane if kind != "from_y" else "core_y")
+        return pltpu.make_async_remote_copy(
+            src_ref=source,
+            dst_ref=target,
+            send_sem=send_sem.at[part, shard, send],
+            recv_sem=recv_sem.at[part, shard, arrive],
+            device_id=peer,
+            device_id_type=MESH,
+        )
+
+    def landed(part, shard, kind):
+        at = window(part, shard, kind)
+        target = full[part].at[at]
+        arrive = {"own": 0, "from_y": 1, "core_own": 2, "core_y": 3}[kind]
+        return pltpu.make_async_remote_copy(
+            src_ref=target,
+            dst_ref=target,
+            send_sem=send_sem.at[part, shard, 0],
+            recv_sem=recv_sem.at[part, shard, arrive],
+            device_id=peer_core,
+            device_id_type=MESH,
+        )
+
+    def pass_on(part, shard):
+        transfer(part, shard, "to_y", "y", peer_y).start()
+        transfer(part, shard, "own", "core", peer_core).start()
+
+    def from_partner(part, row):
+        shard = 2 * row + 1 - x
+        landed(part, shard, "own").wait_recv()
+        pass_on(part, shard)
+
+    def from_y(part, shard):
+        landed(part, shard, "from_y").wait_recv()
+        transfer(part, shard, "from_y", "core", peer_core).start()
+
+    def stage(part, d):
+        if d == 0:
+            @pl.when(has_above)
+            def _():
+                transfer(part, w, "own", "up", above, own=True).start()
+
+            @pl.when(has_below)
+            def _():
+                transfer(part, w, "own", "down", below, own=True).start()
+
+            transfer(part, w, "own", "x", peer_x, own=True).start()
+            pltpu.make_async_copy(mine[part], full[part].at[w], own_sem.at[part]).start()
+            return
+
+        @pl.when(z >= d)
+        def _():
+            shard = w - 2 * d
+            landed(part, shard, "own").wait_recv()
+
+            @pl.when(has_above)
+            def _():
+                transfer(part, shard, "own", "up", above).start()
+
+            transfer(part, shard, "own", "x", peer_x).start()
+            pass_on(part, shard)
+
+        @pl.when(z + d < depth)
+        def _():
+            shard = w + 2 * d
+            landed(part, shard, "own").wait_recv()
+
+            @pl.when(has_below)
+            def _():
+                transfer(part, shard, "own", "down", below).start()
+
+            transfer(part, shard, "own", "x", peer_x).start()
+            pass_on(part, shard)
+
+        late(part, d - 1)
+
+    def late(part, d):
+        for sign in (-1, 1) if d else (1,):
+            row = z + sign * d
+
+            @pl.when((row >= 0) & (row < depth))
+            def _():
+                from_partner(part, row)
+        if d >= 1:
+            later(part, d - 1)
+
+    def later(part, d):
+        for sign in (-1, 1) if d else (1,):
+            row = z + sign * d
+
+            @pl.when((row >= 0) & (row < depth))
+            def _():
+                if d:
+                    from_y(part, 2 * row + x)
+                from_y(part, 2 * row + 1 - x)
+
+    for tick in range(count + depth + 1):
+        for part in range(count):
+            d = tick - part
+            if 0 <= d < depth:
+                stage(part, d)
+            elif d == depth:
+                late(part, d - 1)
+            elif d == depth + 1:
+                later(part, d - 2 + 0)
+
+    for part in range(count):
+        pltpu.make_async_copy(mine[part], full[part].at[w], own_sem.at[part]).wait()
+        for row in range(depth):
+            for side in range(2):
+                shard = 2 * row + side
+
+                @pl.when(shard != w)
+                def _():
+                    landed(part, shard, "core_own").wait_recv()
+                    landed(part, shard, "core_y").wait_recv()
+                    transfer(part, shard, "to_y", "y", peer_y).wait_send()
+                    transfer(part, shard, "own", "core", peer_core).wait_send()
+                    transfer(part, shard, "from_y", "core", peer_core).wait_send()
+
+                @pl.when(side == x)
+                def _():
+                    transfer(part, shard, "own", "x", peer_x).wait_send()
+
+                    @pl.when(has_above & (row <= z))
+                    def _():
+                        transfer(part, shard, "own", "up", above).wait_send()
+
+                    @pl.when(has_below & (row >= z))
+                    def _():
+                        transfer(part, shard, "own", "down", below).wait_send()
+
+
+def gather_weights(parts):
+    wide, narrow = lax.axis_size("wide"), lax.axis_size("narrow")
+    shapes = [part.shape for part in parts]
+    count = len(parts)
+    return pl.pallas_call(
+        functools.partial(gather_kernel, wide, narrow, shapes),
+        out_shape=[jax.ShapeDtypeStruct((wide,) + shape, jnp.bfloat16) for shape in shapes],
+        in_specs=[pl.BlockSpec(memory_space=pl.ANY)] * count,
+        out_specs=[pl.BlockSpec(memory_space=pl.ANY)] * count,
+        scratch_shapes=[
+            pltpu.SemaphoreType.DMA((count,)),
+            pltpu.SemaphoreType.DMA((count, wide, 6)),
+            pltpu.SemaphoreType.DMA((count, wide, 4)),
+        ],
+        compiler_params=pltpu.CompilerParams(collective_id=0, has_side_effects=True),
+    )(*parts)
 
 
 def shifted(x, axis, by):
@@ -34,26 +244,27 @@
     row_count = current.shape[1]
     col_count = current.shape[2]
     chan_count = current.shape[3]
-    block_cols = lax.all_gather(weight, "wide", axis=1, tiled=True)
-    summed = jnp.zeros((row_count * col_count, block_cols.shape[1]), jnp.float32)
+    summed = jnp.zeros((row_count * col_count, weight.shape[0]), jnp.float32)
     for kernel_tap in range(27):
         time_step = kernel_tap // 9
         row_step = kernel_tap // 3 % 3
         col_step = kernel_tap % 3
         window = padded[time_step, row_step : row_step + row_count, col_step : col_step + col_count]
         window = window.reshape(row_count * col_count, chan_count)
-        summed = summed + jnp.dot(
+        summed = summed + lax.dot_general(
             window,
-            block_cols[kernel_tap * chan_count : (kernel_tap + 1) * chan_count],
+            weight[:, kernel_tap * chan_count : (kernel_tap + 1) * chan_count],
+            (((1,), (1,)), ((), ())),
             preferred_element_type=jnp.float32,
         )
     return summed
 
 
 def embed_tokens(patch_feats, embed_weight):
-    return jnp.dot(
+    return lax.dot_general(
         patch_feats,
-        lax.all_gather(embed_weight, "wide", axis=1, tiled=True),
+        embed_weight,
+        (((1,), (1,)), ((), ())),
         preferred_element_type=jnp.float32,
     ).astype(jnp.bfloat16)
 
@@ -62,6 +273,10 @@
     row_count = latent.shape[1]
     col_count = latent.shape[2]
     chan_count = latent.shape[3]
+    conv_first, conv_second, embed_weight = (
+        part.reshape(-1, part.shape[2])
+        for part in gather_weights([conv_first.T, conv_second.T, embed_weight.T])
+    )
     first = causal_conv(latent, conv_first)
     activated = jax.nn.silu(first).astype(jnp.bfloat16).reshape(latent.shape)
     second = causal_conv(activated, conv_second) + latent.reshape(-1, chan_count).astype(

time: 301 us -> 196 us (0.65)
  waiting for transfers between devices: 200 us -> 46.2 us
  Pallas kernels: 0 us -> 59.8 us
  matrix products: 41 us -> 31.5 us
    all_gather x3 -> x0, waiting for transfers between devices: 155 us -> none  [the longest x2 88.1 us: causal_conv(): block_cols = lax.all_gather(weight, 'wide', axis=1, tiled=True)]
    pallas_call x0 -> x1, Pallas kernels: none -> 59.8 us  [gather_weights(): pl.pallas_call(functools.partial(gather_kernel, wide, narrow, shapes), ou...]
    dot_general x55, matrix products: 27.2 us -> 17.7 us  [the longest x54 13.1 us: causal_conv(): lax.dot_general(window, weight[:, kernel_tap * chan_count:(kernel_tap + 1...]
    all_gather x1, waiting for transfers between devices: 19 us -> 26.7 us  [per_device(): lax.all_gather(embed_tokens(patches, embed_weight), 'narrow', axis=0, til...]
    ppermute x2, waiting for transfers between devices: 3.49 us -> 0.01 us  [extended(): lax.ppermute(lax.slice_in_dim(block, 0, width, axis=dim), axis, backward)]
  transfers between devices with their start and end apart: 14 -> 11, of which waited for: 10 -> 8; matrix products, arithmetic and copies ran while one was open for 11% -> 2% of each run, Pallas kernels for 0% -> 31%
where the time goes in v1:
time: 196 us
  Pallas kernels  59.8 us (31%)
  waiting for transfers between devices  46.2 us (24%)
  matrix products  31.5 us (16%)
  starting transfers between devices  31.2 us (16%)
  between operations  14.1 us (7%)
  local copies, waits for them, and re-layouts  8.93 us (5%)
  other arithmetic  4.01 us (2%)
    pallas_call x1, Pallas kernels, gather_weights(): pl.pallas_call(functools.partial(gather_kernel, wide, narrow, shapes), ou...  59.8 us
    all_gather x1, waiting for transfers between devices, per_device(): lax.all_gather(embed_tokens(patches, embed_weight), 'narrow', axis=0, til...  26.7 us
    ppermute x4, starting transfers between devices, shifted(): return lax.ppermute(x, axis, pairs)  15 us
    dot_general x54, matrix products, causal_conv(): lax.dot_general(window, weight[:, kernel_tap * chan_count:(kernel_tap + 1...  13.1 us
    ppermute x4, waiting for transfers between devices, shifted(): return lax.ppermute(x, axis, pairs)  8.51 us
    all_to_all x1, waiting for transfers between devices, per_device(): lax.all_to_all(partial_sums.astype(jnp.bfloat16), 'wide', split_axis=0, c...  6.35 us
    all_to_all x1, starting transfers between devices, per_device(): lax.all_to_all(piece_grid.astype(jnp.bfloat16), 'wide', split_axis=0, con...  5.52 us
    unnamed x14, local copies, waits for them, and re-layouts  4.89 us
  transfers between devices with their start and end apart: 11, of which 8 were waited for; matrix products, arithmetic and copies ran while one was open for 2% of the time, Pallas kernels for 31%

profile of v1, /device:TPU:0, one launch (start us, length us, event | category | flops | bytes accessed | tf_op | source)
XLA Modules:
  0.0 195.7 jit_solution(14074172449820850379)
XLA Ops:
  6.5 4.9 %collective-permute-start = (bf16[1,8,48,256]{3,2,1,0:T(8,128)(2,1)}, bf16[1,8,48,256]{3,2,1,0:T(8,128)(2,1)S(1)}, u32[]{:S(2)}, u32[]{:S(2)}) collective-permute-start(bf16[1,8,48,256]{3,2,1,0:T(8,128)(2,1)} %param.5), channel_id=1, source_target_pairs={{0,8},{4,12},{8,16},{12,20},{16,24},{20,28},{1,9},{5,13},{9,17},{1... | collective-permute-start | bytes 589832 | tf_op jit(solution)/shard_map/ppermute | solution.py:222
  11.5 3.4 %collective-permute-start.1 = (bf16[1,8,48,256]{3,2,1,0:T(8,128)(2,1)}, bf16[1,8,48,256]{3,2,1,0:T(8,128)(2,1)S(1)}, u32[]{:S(2)}, u32[]{:S(2)}) collective-permute-start(bf16[1,8,48,256]{3,2,1,0:T(8,128)(2,1)} %param.5), channel_id=1, source_target_pairs={{0,4},{4,8},{8,12},{12,16},{16,20},{20,24},{24,28},{1,5},{5,9},{9,... | collective-permute-start | bytes 589832 | tf_op jit(solution)/shard_map/ppermute | solution.py:222
  14.9 1.0 collective-permute-done
  15.9 3.1 %collective-permute-done.1 = bf16[1,8,48,256]{3,2,1,0:T(8,128)(2,1)S(1)} collective-permute-done((bf16[1,8,48,256]{3,2,1,0:T(8,128)(2,1)}, bf16[1,8,48,256]{3,2,1,0:T(8,128)(2,1)S(1)}, u32[]{:S(2)}, u32[]{:S(2)}) %collective-permute-start.1) | collective-permute-done | bytes 196640 | tf_op jit(solution)/shard_map/ppermute | solution.py:222
  19.1 0.9 constant_dynamic-update-slice_fusion
  20.0 1.3 collective-permute-start.2
  21.3 1.3 collective-permute-start.3
  22.6 59.8 %shard_map.55 = (bf16[8,32,6912]{2,1,0:T(8,128)(2,1)}, bf16[8,32,6912]{2,1,0:T(8,128)(2,1)}, bf16[8,280,1024]{2,1,0:T(8,128)(2,1)}) custom-call(bf16[32,6912]{1,0:T(8,128)(2,1)} %bitcast.311, bf16[32,6912]{1,0:T(8,128)(2,1)} %bitcast.312, bf16[280,1024]{1,0:T(8,128)(2,1)} %bitcast.309), custom_call_target="tpu_custom_call" | custom-call | tf_op jit(solution)/shard_map/pallas_call | solution.py:205
  83.5 1.5 copy-done.1
  91.8 3.2 %collective-permute-start.4 = (bf16[1,8,48,256]{3,2,1,0:T(8,128)(2,1)S(1)}, bf16[1,8,48,256]{3,2,1,0:T(8,128)(2,1)S(1)}, u32[]{:S(2)}, u32[]{:S(2)}) collective-permute-start(bf16[1,8,48,256]{3,2,1,0:T(8,128)(2,1)S(1)} %bitcast.191), channel_id=1, source_target_pairs={{0,8},{4,12},{8,16},{12,20},{16,24},{20,28},{1,9},{5,13},{9,17},{1... | collective-permute-start | bytes 589832 | tf_op jit(solution)/shard_map/ppermute | solution.py:222
  94.9 3.5 %collective-permute-start.5 = (bf16[1,8,48,256]{3,2,1,0:T(8,128)(2,1)S(1)}, bf16[1,8,48,256]{3,2,1,0:T(8,128)(2,1)S(1)}, u32[]{:S(2)}, u32[]{:S(2)}) collective-permute-start(bf16[1,8,48,256]{3,2,1,0:T(8,128)(2,1)S(1)} %bitcast.192), channel_id=1, source_target_pairs={{0,4},{4,8},{8,12},{12,16},{16,20},{20,24},{24,28},{1,5},{5,9},{9,... | collective-permute-start | bytes 589832 | tf_op jit(solution)/shard_map/ppermute | solution.py:222
  98.5 1.1 collective-permute-done.4
  99.6 3.2 %collective-permute-done.5 = bf16[1,8,48,256]{3,2,1,0:T(8,128)(2,1)S(1)} collective-permute-done((bf16[1,8,48,256]{3,2,1,0:T(8,128)(2,1)S(1)}, bf16[1,8,48,256]{3,2,1,0:T(8,128)(2,1)S(1)}, u32[]{:S(2)}, u32[]{:S(2)}) %collective-permute-start.5) | collective-permute-done | bytes 196640 | tf_op jit(solution)/shard_map/ppermute | solution.py:222
  102.9 1.3 collective-permute-start.7
  104.2 3.2 %collective-permute-start.6 = (bf16[3,1,48,256]{3,2,1,0:T(8,128)(2,1)S(1)}, bf16[3,1,48,256]{3,2,1,0:T(8,128)(2,1)S(1)}, u32[]{:S(2)}, u32[]{:S(2)}) collective-permute-start(bf16[3,1,48,256]{3,2,1,0:T(8,128)(2,1)S(1)} %get-tuple-element.59), channel_id=1, source_target_pairs={{0,1},{1,2},{2,3},{4,5},{5,6},{6,7},{8,9},{9,10},{10,11},{12,13},{... | collective-permute-start | bytes 221192 | tf_op jit(solution)/shard_map/ppermute | solution.py:230
  107.4 0.7 collective-permute-done.6
  109.1 1.5 copy-done
  117.8 4.6 %convolution_convert_fusion.1 = bf16[96,2240]{1,0:T(8,128)(2,1)} fusion(bf16[96,1024]{1,0:T(8,128)(2,1)S(1)} %reshape.77, bf16[2240,1024]{1,0:T(8,128)(2,1)} %bitcast.199), kind=kOutput, calls=%fused_computation.2 | convolution fusion | flops 440616960 | bytes 5214208 | tf_op jit(solution)/shard_map/dot_general | solution.py:264
  122.5 26.7 %all-gather.2.cloned.1.call-done = bf16[384,2240]{1,0:T(8,128)(2,1)} async-done(((bf16[96,2240]{1,0:T(8,128)(2,1)}), bf16[384,2240]{1,0:T(8,128)(2,1)}) %all-gather.2.cloned.1.call-update) | async-done | bytes 1720336 | tf_op jit(solution)/shard_map/all_gather | solution.py:288
  149.2 4.2 %fusion.143 = (bf16[560]{0:T(1024)(128)(2,1)S(1)}, bf16[384,560]{0,1:T(8,128)(2,1)S(1)}) fusion(bf16[384,2240]{1,0:T(8,128)(2,1)} %all-gather.2.cloned.1.call-done, bf16[3,2240,560]{1,2,0:T(8,128)(2,1)} %param.9), kind=kOutput, calls=%fused_computation.211 | convolution fusion | flops 964668864 | bytes 4781152 | tf_op jit(solution)/shard_map/dot_general | solution.py:292
  153.4 3.2 %fusion.17 = bf16[384,560]{0,1:T(8,128)(2,1)S(1)} fusion(bf16[384,2240]{1,0:T(8,128)(2,1)S(1)} %copy-done.3, bf16[3,2240,560]{1,2,0:T(8,128)(2,1)} %param.9), kind=kOutput, calls=%fused_computation.27 | convolution fusion | flops 963594240 | bytes 4730880 | tf_op jit(solution)/shard_map/dot_general | solution.py:293
  158.0 1.4 reduce.5
  159.4 0.8 reshape.90
  160.2 5.5 %all-to-all-start = ((bf16[8,2,3955]{2,1,0:T(2,128)(2,1)}), bf16[8,2,3955]{2,1,0:T(2,128)(2,1)S(1)}, u32[]{:S(2)}, u32[]{:S(2)}) async-start(bf16[8,2,3955]{2,1,0:T(2,128)(2,1)} %reshape.90), calls=%async_computation | async-start | bytes 253952 | tf_op jit(solution)/shard_map/all_to_all | solution.py:330
  165.7 3.4 %fusion.44 = bf16[384,560]{0,1:T(8,128)(2,1)S(1)} fusion(bf16[384,2240]{1,0:T(8,128)(2,1)S(1)} %copy-done.3, bf16[3,2240,560]{1,2,0:T(8,128)(2,1)} %param.9), kind=kOutput, calls=%fused_computation.89 | convolution fusion | flops 964454400 | bytes 4730880 | tf_op jit(solution)/shard_map/dot_general | solution.py:291
  169.1 3.9 %all-to-all-done = bf16[8,2,3955]{2,1,0:T(2,128)(2,1)S(1)} async-done(((bf16[8,2,3955]{2,1,0:T(2,128)(2,1)}), bf16[8,2,3955]{2,1,0:T(2,128)(2,1)S(1)}, u32[]{:S(2)}, u32[]{:S(2)}) %all-to-all-start) | async-done | bytes 126592 | tf_op jit(solution)/shard_map/all_to_all | solution.py:330
  174.0 0.8 reshape.92
  174.8 3.6 %all-to-all-start.1 = ((bf16[8,2,3955]{2,1,0:T(2,128)(2,1)}), bf16[8,2,3955]{2,1,0:T(2,128)(2,1)S(1)}, u32[]{:S(2)}, u32[]{:S(2)}) async-start(bf16[8,2,3955]{2,1,0:T(2,128)(2,1)} %reshape.92), calls=%async_computation.1 | async-start | bytes 253952 | tf_op jit(solution)/shard_map/all_to_all | solution.py:335
  178.4 0.7 select_reduce_fusion
  179.1 6.3 %all-to-all-done.1 = bf16[8,2,3955]{2,1,0:T(2,128)(2,1)S(1)} async-done(((bf16[8,2,3955]{2,1,0:T(2,128)(2,1)}), bf16[8,2,3955]{2,1,0:T(2,128)(2,1)S(1)}, u32[]{:S(2)}, u32[]{:S(2)}) %all-to-all-start.1) | async-done | bytes 126592 | tf_op jit(solution)/shard_map/all_to_all | solution.py:335
  185.6 0.7 reduce.2
  187.6 1.3 fusion.20
  (96 shorter events, 19.4 us)
Async XLA Ops:
  6.5 142.6 %all-gather.2.cloned.1.call-start = ((), (), s32[]{:S(2)}) async-start(), calls=%async_computation.2 | async-start | bytes 2211840 | tf_op jit(solution)/shard_map/all_gather | solution.py:288
  6.5 9.4 %collective-permute-start = (bf16[1,8,48,256]{3,2,1,0:T(8,128)(2,1)}, bf16[1,8,48,256]{3,2,1,0:T(8,128)(2,1)S(1)}, u32[]{:S(2)}, u32[]{:S(2)}) collective-permute-start(bf16[1,8,48,256]{3,2,1,0:T(8,128)(2,1)} %param.5), channel_id=1, source_target_pairs={{0,8},{4,12},{8,16},{12,20},{16,24},{20,28},{1,9},{5,13},{9,17},{1... | collective-permute-start | bytes 589832 | tf_op jit(solution)/shard_map/ppermute | solution.py:222
  11.5 7.6 %collective-permute-start.1 = (bf16[1,8,48,256]{3,2,1,0:T(8,128)(2,1)}, bf16[1,8,48,256]{3,2,1,0:T(8,128)(2,1)S(1)}, u32[]{:S(2)}, u32[]{:S(2)}) collective-permute-start(bf16[1,8,48,256]{3,2,1,0:T(8,128)(2,1)} %param.5), channel_id=1, source_target_pairs={{0,4},{4,8},{8,12},{12,16},{16,20},{20,24},{24,28},{1,5},{5,9},{9,... | collective-permute-start | bytes 589832 | tf_op jit(solution)/shard_map/ppermute | solution.py:222
  20.0 62.4 %collective-permute-start.2 = (bf16[3,1,48,256]{3,2,1,0:T(8,128)(2,1)S(1)}, bf16[3,1,48,256]{3,2,1,0:T(8,128)(2,1)S(1)}, u32[]{:S(2)}, u32[]{:S(2)}) collective-permute-start(bf16[3,1,48,256]{3,2,1,0:T(8,128)(2,1)S(1)} %get-tuple-element.64), channel_id=1, source_target_pairs={{0,1},{1,2},{2,3},{4,5},{5,6},{6,7},{8,9},{9,10},{10,11},{12,13},{... | collective-permute-start | bytes 221192 | tf_op jit(solution)/shard_map/ppermute | solution.py:230
  21.3 61.1 %collective-permute-start.3 = (bf16[3,1,48,256]{3,2,1,0:T(8,128)(2,1)S(1)}, bf16[3,1,48,256]{3,2,1,0:T(8,128)(2,1)S(1)}, u32[]{:S(2)}, u32[]{:S(2)}) collective-permute-start(bf16[3,1,48,256]{3,2,1,0:T(8,128)(2,1)S(1)} %get-tuple-element.65), channel_id=1, source_target_pairs={{1,0},{2,1},{3,2},{5,4},{6,5},{7,6},{9,8},{10,9},{11,10},{13,12},{... | collective-permute-start | bytes 221192 | tf_op jit(solution)/shard_map/ppermute | solution.py:233
  82.9 2.0 %copy-start.1 = (bf16[8,32,6912]{2,1,0:T(8,128)(2,1)S(1)}, bf16[8,32,6912]{2,1,0:T(8,128)(2,1)}, u32[]{:S(2)}) copy-start(bf16[8,32,6912]{2,1,0:T(8,128)(2,1)} %get-tuple-element.8) | copy-start | bytes 10616836
  89.2 1.5 copy-start.2
  91.8 7.8 %collective-permute-start.4 = (bf16[1,8,48,256]{3,2,1,0:T(8,128)(2,1)S(1)}, bf16[1,8,48,256]{3,2,1,0:T(8,128)(2,1)S(1)}, u32[]{:S(2)}, u32[]{:S(2)}) collective-permute-start(bf16[1,8,48,256]{3,2,1,0:T(8,128)(2,1)S(1)} %bitcast.191), channel_id=1, source_target_pairs={{0,8},{4,12},{8,16},{12,20},{16,24},{20,28},{1,9},{5,13},{9,17},{1... | collective-permute-start | bytes 589832 | tf_op jit(solution)/shard_map/ppermute | solution.py:222
  94.9 7.9 %collective-permute-start.5 = (bf16[1,8,48,256]{3,2,1,0:T(8,128)(2,1)S(1)}, bf16[1,8,48,256]{3,2,1,0:T(8,128)(2,1)S(1)}, u32[]{:S(2)}, u32[]{:S(2)}) collective-permute-start(bf16[1,8,48,256]{3,2,1,0:T(8,128)(2,1)S(1)} %bitcast.192), channel_id=1, source_target_pairs={{0,4},{4,8},{8,12},{12,16},{16,20},{20,24},{24,28},{1,5},{5,9},{9,... | collective-permute-start | bytes 589832 | tf_op jit(solution)/shard_map/ppermute | solution.py:222
  102.9 4.5 %collective-permute-start.7 = (bf16[3,1,48,256]{3,2,1,0:T(8,128)(2,1)S(1)}, bf16[3,1,48,256]{3,2,1,0:T(8,128)(2,1)S(1)}, u32[]{:S(2)}, u32[]{:S(2)}) collective-permute-start(bf16[3,1,48,256]{3,2,1,0:T(8,128)(2,1)S(1)} %get-tuple-element.60), channel_id=1, source_target_pairs={{1,0},{2,1},{3,2},{5,4},{6,5},{7,6},{9,8},{10,9},{11,10},{13,12},{... | collective-permute-start | bytes 221192 | tf_op jit(solution)/shard_map/ppermute | solution.py:233
  104.2 3.9 %collective-permute-start.6 = (bf16[3,1,48,256]{3,2,1,0:T(8,128)(2,1)S(1)}, bf16[3,1,48,256]{3,2,1,0:T(8,128)(2,1)S(1)}, u32[]{:S(2)}, u32[]{:S(2)}) collective-permute-start(bf16[3,1,48,256]{3,2,1,0:T(8,128)(2,1)S(1)} %get-tuple-element.59), channel_id=1, source_target_pairs={{0,1},{1,2},{2,3},{4,5},{5,6},{6,7},{8,9},{9,10},{10,11},{12,13},{... | collective-permute-start | bytes 221192 | tf_op jit(solution)/shard_map/ppermute | solution.py:230
  108.6 2.0 %copy-start = (bf16[8,32,6912]{2,1,0:T(8,128)(2,1)S(1)}, bf16[8,32,6912]{2,1,0:T(8,128)(2,1)}, u32[]{:S(2)}) copy-start(bf16[8,32,6912]{2,1,0:T(8,128)(2,1)} %get-tuple-element.9) | copy-start | bytes 10616836
  149.2 4.2 %copy-start.3 = (bf16[384,2240]{1,0:T(8,128)(2,1)S(1)}, bf16[384,2240]{1,0:T(8,128)(2,1)}, u32[]{:S(2)}) copy-start(bf16[384,2240]{1,0:T(8,128)(2,1)} %all-gather.2.cloned.1.call-done) | copy-start | bytes 5160964
  160.2 12.8 %all-to-all-start = ((bf16[8,2,3955]{2,1,0:T(2,128)(2,1)}), bf16[8,2,3955]{2,1,0:T(2,128)(2,1)S(1)}, u32[]{:S(2)}, u32[]{:S(2)}) async-start(bf16[8,2,3955]{2,1,0:T(2,128)(2,1)} %reshape.90), calls=%async_computation | async-start | bytes 253952 | tf_op jit(solution)/shard_map/all_to_all | solution.py:330
  174.8 10.6 %all-to-all-start.1 = ((bf16[8,2,3955]{2,1,0:T(2,128)(2,1)}), bf16[8,2,3955]{2,1,0:T(2,128)(2,1)S(1)}, u32[]{:S(2)}, u32[]{:S(2)}) async-start(bf16[8,2,3955]{2,1,0:T(2,128)(2,1)} %reshape.92), calls=%async_computation.1 | async-start | bytes 253952 | tf_op jit(solution)/shard_map/all_to_all | solution.py:335
Sparse Core Ops, SparseCore 0:
  122.5 26.5 all-gather.1

commit v2 on v1

--- a/solution.py
+++ b/solution.py
@@ -17,10 +17,18 @@
     return half, max(1, half // 3)
 
 
-def gather_kernel(wide, narrow, shapes, *refs):
+def block_kernel(
+    wide, narrow, shapes, latent, first_w, second_w, embed_w, patches, embed_full,
+    first_full, second_full, frames, halo_out, columns, total, lanes, own_sem, send_sem, recv_sem,
+    edge_send, edge_recv, strip_send, strip_recv,
+):
     count = len(shapes)
-    mine, full = refs[:count], refs[count : 2 * count]
-    own_sem, send_sem, recv_sem = refs[2 * count :]
+    mine = (first_w, second_w, embed_w)
+    full = (first_full, second_full, embed_full)
+    rows, cols, chans = latent.shape[1:]
+    frames[...] = jnp.zeros_like(frames)
+    halo_out[...] = jnp.zeros_like(halo_out)
+    frames[2, 1 : rows + 1] = latent[0]
     w = lax.axis_index("wide")
     n = lax.axis_index("narrow")
     z, x = w // 2, lax.rem(w, 2)
@@ -44,7 +52,142 @@
     def _():
         pl.semaphore_signal(barrier, inc=1, device_id=below, device_id_type=MESH)
 
-    pl.semaphore_wait(barrier, 3 + has_above.astype(jnp.int32) + has_below.astype(jnp.int32))
+    def inside(frame, strip):
+        return (frame >= 0) & (frame < wide) & (strip >= 0) & (strip < narrow)
+
+    edges = [(j, i) for j in (2, 1, 0) for i in (0, -1, 1) if (j, i) != (0, 0)]
+    expected = 3 + has_above.astype(jnp.int32) + has_below.astype(jnp.int32)
+    for j, i in edges:
+        @pl.when(inside(w - j, n - i))
+        def _():
+            pl.semaphore_signal(
+                barrier, inc=1, device_id={"wide": w - j, "narrow": n - i}, device_id_type=MESH
+            )
+
+        expected = expected + inside(w + j, n + i).astype(jnp.int32)
+    pl.semaphore_wait(barrier, expected)
+
+    def edge_copy(which, index, toward=1):
+        j, i = edges[index]
+        ref = (frames, halo_out)[which]
+        if i == 0:
+            source, target = pl.ds(1, rows), pl.ds(1, rows)
+        elif i == 1:
+            source, target = pl.ds(rows, 1), pl.ds(0, 1)
+        else:
+            source, target = pl.ds(1, 1), pl.ds(rows + 1, 1)
+        return pltpu.make_async_remote_copy(
+            src_ref=ref.at[2, source],
+            dst_ref=ref.at[2 - j, target],
+            send_sem=edge_send.at[which, index],
+            recv_sem=edge_recv.at[which, index],
+            device_id={"wide": w + toward * j, "narrow": n + toward * i},
+            device_id_type=MESH,
+        )
+
+    def send_edges(which):
+        for index, (j, i) in enumerate(edges):
+            @pl.when(inside(w + j, n + i))
+            def _():
+                edge_copy(which, index).start()
+
+    def fill_columns(which):
+        for index, (j, i) in enumerate(edges):
+            @pl.when(inside(w - j, n - i))
+            def _():
+                edge_copy(which, index, -1).wait_recv()
+        ref = (frames, halo_out)[which]
+        place = lax.broadcasted_iota(jnp.int32, (rows + 2, cols, chans), 1)
+        place = place.reshape((rows + 2) * cols, chans)
+        for a in range(3):
+            flat = ref[a].reshape((rows + 2) * cols, chans)
+            wider = flat.astype(jnp.float32)
+            for e in range(3):
+                if e == 0:
+                    moved = jnp.where(place == 0, 0.0, pltpu.roll(wider, 1, 0))
+                    moved = moved.astype(jnp.bfloat16)
+                elif e == 1:
+                    moved = flat
+                else:
+                    moved = pltpu.roll(wider, (rows + 2) * cols - 1, 0)
+                    moved = jnp.where(place == cols - 1, 0.0, moved).astype(jnp.bfloat16)
+                for b in range(3):
+                    tap = 9 * a + 3 * b + e
+                    columns[:, tap * chans : (tap + 1) * chans] = moved[
+                        b * cols : (b + rows) * cols
+                    ]
+
+    def convolve(part):
+        outs = wide * shapes[part][0]
+        size = 3 * chans
+        total[...] = jnp.zeros_like(total)
+
+        def step(index, carry):
+            at = pl.ds(pl.multiple_of(index * size, LANE), size)
+            total[...] += lax.dot_general(
+                columns[:, at],
+                full[part][:, :, at].reshape(outs, size),
+                (((1,), (1,)), ((), ())),
+                preferred_element_type=jnp.float32,
+            )
+            return carry
+
+        lax.fori_loop(0, 9, step, 0)
+
+    strip_tokens = rows * cols // 4
+
+    def strip_copy(kind):
+        strip = {"core": n, "y": n, "relay": n + 2 - 4 * y}[kind]
+        index = ("core", "y", "relay").index(kind)
+        return pltpu.make_async_remote_copy(
+            src_ref=patches.at[strip],
+            dst_ref=patches.at[strip],
+            send_sem=strip_send.at[index],
+            recv_sem=strip_recv.at[index],
+            device_id=peer_y if kind == "y" else peer_core,
+            device_id_type=MESH,
+        )
+
+    def strip_landed(kind):
+        strip = {"core": n + 1 - 2 * core, "y": n + 2 - 4 * y, "relay": 3 - n}[kind]
+        index = ("core", "y", "relay").index(kind)
+        return pltpu.make_async_remote_copy(
+            src_ref=patches.at[strip],
+            dst_ref=patches.at[strip],
+            send_sem=strip_send.at[index],
+            recv_sem=strip_recv.at[index],
+            device_id=peer_y if kind == "y" else peer_core,
+            device_id_type=MESH,
+        )
+
+    def first_conv():
+        complete(0)
+        convolve(0)
+        outcome = total[...]
+        outcome = outcome / (1.0 + jnp.exp(-outcome))
+        halo_out[2, 1 : rows + 1] = outcome.astype(jnp.bfloat16).reshape(rows, cols, chans)
+        send_edges(1)
+
+    def second_conv():
+        fill_columns(1)
+        complete(1)
+        convolve(1)
+        result = total[...] + latent[0].reshape(rows * cols, chans).astype(jnp.float32)
+        for part in range(chans // LANE):
+            lanes[part] = result[:, part * LANE : (part + 1) * LANE]
+        for b in range(2):
+            for e in range(2):
+                for part in range(chans // LANE):
+                    pieces = [
+                        lanes[part, pl.ds((2 * p + b) * cols + e, cols // 2, stride=2), :]
+                        for p in range(rows // 2)
+                    ]
+                    at = (2 * b + e) * chans + part * LANE
+                    patches[n, :, at : at + LANE] = jnp.concatenate(pieces, axis=0).astype(
+                        jnp.bfloat16
+                    )
+        strip_copy("core").start()
+        strip_copy("y").start()
 
     def window(part, shard, kind):
         half, third = strips(shapes[part][1])
@@ -161,26 +304,50 @@
                     from_y(part, 2 * row + x)
                 from_y(part, 2 * row + 1 - x)
 
-    for tick in range(count + depth + 1):
+    def complete(part):
+        pltpu.make_async_copy(mine[part], full[part].at[w], own_sem.at[part]).wait()
+        for shard in range(wide):
+            @pl.when(shard != w)
+            def _():
+                landed(part, shard, "core_own").wait_recv()
+                landed(part, shard, "core_y").wait_recv()
+
+    for tick in range(2 * count + depth):
         for part in range(count):
-            d = tick - part
+            d = tick - 2 * part
             if 0 <= d < depth:
                 stage(part, d)
             elif d == depth:
                 late(part, d - 1)
             elif d == depth + 1:
-                later(part, d - 2 + 0)
-
+                later(part, d - 2)
+        if tick == 0:
+            send_edges(0)
+        if tick == 2:
+            fill_columns(0)
+        if tick == depth + 1:
+            first_conv()
+        if tick == depth + 3:
+            second_conv()
+    strip_landed("y").wait_recv()
+    strip_copy("relay").start()
+    complete(2)
+    strip_landed("core").wait_recv()
+    strip_landed("relay").wait_recv()
+    for kind in ("core", "y", "relay"):
+        strip_copy(kind).wait_send()
+    for which in range(2):
+        for index, (j, i) in enumerate(edges):
+            @pl.when(inside(w + j, n + i))
+            def _():
+                edge_copy(which, index).wait_send()
     for part in range(count):
-        pltpu.make_async_copy(mine[part], full[part].at[w], own_sem.at[part]).wait()
         for row in range(depth):
             for side in range(2):
                 shard = 2 * row + side
 
                 @pl.when(shard != w)
                 def _():
-                    landed(part, shard, "core_own").wait_recv()
-                    landed(part, shard, "core_y").wait_recv()
                     transfer(part, shard, "to_y", "y", peer_y).wait_send()
                     transfer(part, shard, "own", "core", peer_core).wait_send()
                     transfer(part, shard, "from_y", "core", peer_core).wait_send()
@@ -198,22 +365,44 @@
                         transfer(part, shard, "own", "down", below).wait_send()
 
 
-def gather_weights(parts):
+def conv_block(latent, parts):
     wide, narrow = lax.axis_size("wide"), lax.axis_size("narrow")
     shapes = [part.shape for part in parts]
     count = len(parts)
+    rows, cols, chans = latent.shape[1:]
+    whole = [(wide,) + shape for shape in shapes]
     return pl.pallas_call(
-        functools.partial(gather_kernel, wide, narrow, shapes),
-        out_shape=[jax.ShapeDtypeStruct((wide,) + shape, jnp.bfloat16) for shape in shapes],
-        in_specs=[pl.BlockSpec(memory_space=pl.ANY)] * count,
-        out_specs=[pl.BlockSpec(memory_space=pl.ANY)] * count,
+        functools.partial(block_kernel, wide, narrow, shapes),
+        out_shape=[
+            jax.ShapeDtypeStruct((narrow, rows * cols // 4, 4 * chans), jnp.bfloat16),
+            jax.ShapeDtypeStruct(whole[2], jnp.bfloat16),
+        ],
+        in_specs=[pl.BlockSpec(memory_space=pltpu.VMEM)]
+        + [pl.BlockSpec(memory_space=pl.ANY)] * count,
+        out_specs=[
+            pl.BlockSpec(memory_space=pltpu.VMEM),
+            pl.BlockSpec(memory_space=pl.ANY),
+        ],
         scratch_shapes=[
+            pltpu.VMEM(whole[0], jnp.bfloat16),
+            pltpu.VMEM(whole[1], jnp.bfloat16),
+            pltpu.VMEM((3, rows + 2, cols, chans), jnp.bfloat16),
+            pltpu.VMEM((3, rows + 2, cols, chans), jnp.bfloat16),
+            pltpu.VMEM((rows * cols, 27 * chans), jnp.bfloat16),
+            pltpu.VMEM((rows * cols, chans), jnp.float32),
+            pltpu.VMEM((chans // LANE, rows * cols, LANE), jnp.float32),
             pltpu.SemaphoreType.DMA((count,)),
             pltpu.SemaphoreType.DMA((count, wide, 6)),
             pltpu.SemaphoreType.DMA((count, wide, 4)),
+            pltpu.SemaphoreType.DMA((2, 8)),
+            pltpu.SemaphoreType.DMA((2, 8)),
+            pltpu.SemaphoreType.DMA((3,)),
+            pltpu.SemaphoreType.DMA((3,)),
         ],
-        compiler_params=pltpu.CompilerParams(collective_id=0, has_side_effects=True),
-    )(*parts)
+        compiler_params=pltpu.CompilerParams(
+            collective_id=0, has_side_effects=True, vmem_limit_bytes=40 * 1024 * 1024
+        ),
+    )(latent, *parts)
 
 
 def shifted(x, axis, by):
@@ -244,39 +433,34 @@
     row_count = current.shape[1]
     col_count = current.shape[2]
     chan_count = current.shape[3]
-    summed = jnp.zeros((row_count * col_count, weight.shape[0]), jnp.float32)
+    block_cols = lax.all_gather(weight, "wide", axis=1, tiled=True)
+    summed = jnp.zeros((row_count * col_count, block_cols.shape[1]), jnp.float32)
     for kernel_tap in range(27):
         time_step = kernel_tap // 9
         row_step = kernel_tap // 3 % 3
         col_step = kernel_tap % 3
         window = padded[time_step, row_step : row_step + row_count, col_step : col_step + col_count]
         window = window.reshape(row_count * col_count, chan_count)
-        summed = summed + lax.dot_general(
+        summed = summed + jnp.dot(
             window,
-            weight[:, kernel_tap * chan_count : (kernel_tap + 1) * chan_count],
-            (((1,), (1,)), ((), ())),
+            block_cols[kernel_tap * chan_count : (kernel_tap + 1) * chan_count],
             preferred_element_type=jnp.float32,
         )
     return summed
 
 
 def embed_tokens(patch_feats, embed_weight):
-    return lax.dot_general(
+    return jnp.dot(
         patch_feats,
-        embed_weight,
-        (((1,), (1,)), ((), ())),
+        lax.all_gather(embed_weight, "wide", axis=1, tiled=True),
         preferred_element_type=jnp.float32,
     ).astype(jnp.bfloat16)
 
 
-def per_device(latent, conv_first, conv_second, embed_weight, qkv_weight):
+def embedded_plain(latent, conv_first, conv_second, embed_weight):
     row_count = latent.shape[1]
     col_count = latent.shape[2]
     chan_count = latent.shape[3]
-    conv_first, conv_second, embed_weight = (
-        part.reshape(-1, part.shape[2])
-        for part in gather_weights([conv_first.T, conv_second.T, embed_weight.T])
-    )
     first = causal_conv(latent, conv_first)
     activated = jax.nn.silu(first).astype(jnp.bfloat16).reshape(latent.shape)
     second = causal_conv(activated, conv_second) + latent.reshape(-1, chan_count).astype(
@@ -285,7 +469,24 @@
     block_out = second.astype(jnp.bfloat16)
     patches = block_out.reshape(row_count // 2, 2, col_count // 2, 2, chan_count)
     patches = patches.transpose(0, 2, 1, 3, 4).reshape(-1, 4 * chan_count)
-    embedded = lax.all_gather(embed_tokens(patches, embed_weight), "narrow", axis=0, tiled=True)
+    return lax.all_gather(embed_tokens(patches, embed_weight), "narrow", axis=0, tiled=True)
+
+
+def embedded_fused(latent, conv_first, conv_second, embed_weight):
+    patches, weights = conv_block(latent, [conv_first.T, conv_second.T, embed_weight.T])
+    return lax.dot_general(
+        patches.reshape(-1, patches.shape[2]),
+        weights.reshape(-1, weights.shape[2]),
+        (((1,), (1,)), ((), ())),
+        preferred_element_type=jnp.float32,
+    ).astype(jnp.bfloat16)
+
+
+def per_device(latent, conv_first, conv_second, embed_weight, qkv_weight):
+    wide, narrow = lax.axis_size("wide"), lax.axis_size("narrow")
+    fits = narrow == 4 and wide % 2 == 0 and conv_first.shape[1] % 16 == 0
+    embed = embedded_fused if fits else embedded_plain
+    embedded = embed(latent, conv_first, conv_second, embed_weight)
     heads_here = qkv_weight.shape[2] // HEAD_DIM
     token_count = embedded.shape[0]
     query_raw = jnp.dot(embedded, qkv_weight[0], preferred_element_type=jnp.float32)

time: 196 us -> 120 us (0.61)
  waiting for transfers between devices: 46.2 us -> 10.5 us
  matrix products: 31.5 us -> 12.4 us
  starting transfers between devices: 31.2 us -> 15.5 us
  between operations: 14.1 us -> 0.18 us
  Pallas kernels: 59.8 us -> 70.8 us
    all_gather x1 -> x0, waiting for transfers between devices: 26.7 us -> none  [per_device(): lax.all_gather(embed_tokens(patches, embed_weight), 'narrow', axis=0, til...]
    ppermute x8 -> x0, starting transfers between devices: 22.1 us -> none  [the longest x4 15 us: shifted(): return lax.ppermute(x, axis, pairs)]
    dot_general x55 -> x1, matrix products: 17.7 us -> 2.66 us  [embedded_fused(): lax.dot_general(patches.reshape(-1, patches.shape[2]), weights.reshape(-1...]
    pallas_call x1, Pallas kernels: 59.8 us -> 70.8 us  [conv_block(): pl.pallas_call(functools.partial(block_kernel, wide, narrow, shapes), out...]
    ppermute x8 -> x0, waiting for transfers between devices: 9.22 us -> none  [the longest x4 8.51 us: shifted(): return lax.ppermute(x, axis, pairs)]
    all_to_all x1, starting transfers between devices: 5.52 us -> 12.1 us  [per_device(): lax.all_to_all(piece_grid.astype(jnp.bfloat16), 'wide', split_axis=0, con...]
    dot_general x1, matrix products: 4.24 us -> 1.86 us  [per_device(): jnp.dot(embedded, qkv_weight[1], preferred_element_type=jnp.float32)]
    unnamed x14 -> x16, local copies, waits for them, and re-layouts: 4.89 us -> 5.95 us
  transfers between devices with their start and end apart: 11 -> 2, of which waited for: 8 -> 2; matrix products, arithmetic and copies ran while one was open for 2% -> 3% of each run, Pallas kernels for 31% -> 0%
where the time goes in v2:
time: 120 us
  Pallas kernels  70.8 us (59%)
  starting transfers between devices  15.5 us (13%)
  matrix products  12.4 us (10%)
  waiting for transfers between devices  10.5 us (9%)
  local copies, waits for them, and re-layouts  7.61 us (6%)
  other arithmetic  2.7 us (2%)
    pallas_call x1, Pallas kernels, conv_block(): pl.pallas_call(functools.partial(block_kernel, wide, narrow, shapes), out...  70.8 us
    all_to_all x1, starting transfers between devices, per_device(): lax.all_to_all(piece_grid.astype(jnp.bfloat16), 'wide', split_axis=0, con...  12.1 us
    all_to_all x1, waiting for transfers between devices, per_device(): lax.all_to_all(partial_sums.astype(jnp.bfloat16), 'wide', split_axis=0, c...  6.57 us
    unnamed x16, local copies, waits for them, and re-layouts  5.95 us
    all_to_all x1, waiting for transfers between devices, per_device(): lax.all_to_all(piece_grid.astype(jnp.bfloat16), 'wide', split_axis=0, con...  3.95 us
    dot_general x1, matrix products, per_device(): jnp.dot(embedded, qkv_weight[0], preferred_element_type=jnp.float32)  3.44 us
    all_to_all x1, starting transfers between devices, per_device(): lax.all_to_all(partial_sums.astype(jnp.bfloat16), 'wide', split_axis=0, c...  3.37 us
    dot_general x1, matrix products, embedded_fused(): lax.dot_general(patches.reshape(-1, patches.shape[2]), weights.reshape(-1...  2.66 us
  transfers between devices with their start and end apart: 2, of which 2 were waited for; matrix products, arithmetic and copies ran while one was open for 3% of the time, Pallas kernels for 0%

profile of v2, /device:TPU:0, one launch (start us, length us, event | category | flops | bytes accessed | tf_op | source)
XLA Modules:
  0.0 119.6 jit_solution(18152235751206925305)
XLA Ops:
  0.0 1.1 copy-done
  1.1 1.0 copy-done.1
  2.1 1.0 copy-done.2
  3.1 0.9 copy-done.3
  4.0 70.8 %shard_map.55 = (bf16[4,96,1024]{2,1,0:T(8,128)(2,1)S(1)}, bf16[8,280,1024]{2,1,0:T(8,128)(2,1)S(1)}) custom-call(bf16[1,8,48,256]{3,2,1,0:T(8,128)(2,1)S(1)} %copy-done.3, bf16[32,6912]{1,0:T(8,128)(2,1)S(1)} %bitcast.68, bf16[32,6912]{1,0:T(8,128)(2,1)S(1)} %bitcast.69, bf16[280,1024]{1,0:T(8,128)(2,1)S(1)} %bitcast.67), custom_call_target="tpu_custom_call" | custom-call | tf_op jit(solution)/shard_map/pallas_call | solution.py:374
  74.8 2.7 %convolution_convert_fusion.1 = bf16[384,2240]{0,1:T(8,128)(2,1)S(1)} fusion(bf16[384,1024]{1,0:T(8,128)(2,1)S(1)} %bitcast.71, bf16[2240,1024]{1,0:T(8,128)(2,1)S(1)} %bitcast.70), kind=kOutput, calls=%fused_computation.2 | convolution fusion | flops 1762467840 | bytes 7094272 | tf_op jit(solution)/shard_map/dot_general | solution.py:477
  77.5 1.9 %fusion.44 = (bf16[560]{0:T(1024)(128)(2,1)S(1)}, bf16[384,560]{0,1:T(8,128)(2,1)S(1)}) fusion(bf16[384,2240]{0,1:T(8,128)(2,1)S(1)} %convolution_convert_fusion.1, bf16[3,2240,560]{1,2,0:T(8,128)(2,1)S(1)} %bitcast.81), kind=kOutput, calls=%fused_computation.44 | convolution fusion | flops 964668864 | bytes 4732000 | tf_op jit(solution)/shard_map/dot_general | solution.py:493
  79.4 1.5 %fusion.16 = bf16[384,560]{0,1:T(8,128)(2,1)S(1)} fusion(bf16[384,2240]{0,1:T(8,128)(2,1)S(1)} %convolution_convert_fusion.1, bf16[3,2240,560]{1,2,0:T(8,128)(2,1)S(1)} %bitcast.81), kind=kOutput, calls=%fused_computation.24 | convolution fusion | flops 963594240 | bytes 4730880 | tf_op jit(solution)/shard_map/dot_general | solution.py:494
  80.9 0.3 convolution_convert_fusion.2
  81.2 0.3 reshape.64
  81.5 0.2 convert_element_type.49
  81.7 0.5 broadcast.12
  82.2 1.3 %reduce.5 = bf16[8,7910]{1,0:T(8,128)(2,1)S(1)} reduce(bf16[8,1,7910]{2,1,0:T(2,128)(2,1)S(1)} %convert_element_type.49, bf16[]{:T(256)} %broadcast.12), dimensions={1}, to_apply=%convert_element_type.49.reduce_sub_computation | reduce | bytes 253122 | tf_op jit(solution)/shard_map/convert_element_type | solution.py:532
  83.5 0.8 reshape.72
  84.3 12.1 %all-to-all-start = ((bf16[8,2,3955]{2,1,0:T(2,128)(2,1)}), bf16[8,2,3955]{2,1,0:T(2,128)(2,1)S(1)}, u32[]{:S(2)}, u32[]{:S(2)}) async-start(bf16[8,2,3955]{2,1,0:T(2,128)(2,1)} %reshape.72), calls=%async_computation | async-start | bytes 253952 | tf_op jit(solution)/shard_map/all_to_all | solution.py:531
  96.4 3.4 %fusion.26 = bf16[384,560]{0,1:T(8,128)(2,1)S(1)} fusion(bf16[384,2240]{0,1:T(8,128)(2,1)S(1)} %convolution_convert_fusion.1, bf16[3,2240,560]{1,2,0:T(8,128)(2,1)} %param.9), kind=kOutput, calls=%fused_computation.29 | convolution fusion | flops 964454400 | bytes 4730880 | tf_op jit(solution)/shard_map/dot_general | solution.py:492
  99.9 4.0 %all-to-all-done = bf16[8,2,3955]{2,1,0:T(2,128)(2,1)S(1)} async-done(((bf16[8,2,3955]{2,1,0:T(2,128)(2,1)}), bf16[8,2,3955]{2,1,0:T(2,128)(2,1)S(1)}, u32[]{:S(2)}, u32[]{:S(2)}) %all-to-all-start) | async-done | bytes 126592 | tf_op jit(solution)/shard_map/all_to_all | solution.py:531
  103.8 0.2 reshape.73
  104.0 0.2 fusion
  104.2 0.6 reduce.6
  104.8 0.8 reshape.74
  105.6 3.4 %all-to-all-start.1 = ((bf16[8,2,3955]{2,1,0:T(2,128)(2,1)}), bf16[8,2,3955]{2,1,0:T(2,128)(2,1)S(1)}, u32[]{:S(2)}, u32[]{:S(2)}) async-start(bf16[8,2,3955]{2,1,0:T(2,128)(2,1)} %reshape.74), calls=%async_computation.1 | async-start | bytes 253952 | tf_op jit(solution)/shard_map/all_to_all | solution.py:536
  108.9 0.7 select_reduce_fusion
  109.6 6.6 %all-to-all-done.1 = bf16[8,2,3955]{2,1,0:T(2,128)(2,1)S(1)} async-done(((bf16[8,2,3955]{2,1,0:T(2,128)(2,1)}), bf16[8,2,3955]{2,1,0:T(2,128)(2,1)S(1)}, u32[]{:S(2)}, u32[]{:S(2)}) %all-to-all-start.1) | async-done | bytes 126592 | tf_op jit(solution)/shard_map/all_to_all | solution.py:536
  116.2 0.2 reshape.75
  116.4 0.7 reduce.2
  117.1 0.3 slice.22
  117.4 0.2 reshape.65
  117.6 0.2 fusion.41
  117.8 0.2 reshape.66
  118.0 0.3 fusion.45
  118.4 1.3 %fusion.19 = bf16[384,5,112]{0,2,1:T(8,128)(2,1)} fusion(f32[5,112,384]{2,1,0:T(8,128)S(1)} %fusion.45, bf16[384,5,112]{0,2,1:T(8,128)(2,1)S(1)} %bitcast.77, bf16[5,384,384]{1,2,0:T(8,128)(2,1)S(1)} %get-tuple-element.12, pred[384,384]{0,1:T(8,128)(4,1)S(1)} %iota_compare_fusion, f32[384,5]{0,1:T(8,128)S(1)} %fusion.40), kind=kOutput, calls=%fused_computation.25 | convolution fusion | flops 166533120 | bytes 3350016 | tf_op jit(solution)/shard_map/hts,she->the/dot_general | solution.py:511
  (13 shorter events, 0.1 us)
Async XLA Ops:
  0.0 1.1 copy-start
  1.1 1.0 copy-start.1
  2.1 1.0 copy-start.2
  3.1 0.9 copy-start.3
  4.0 73.5 %slice-start = ((s8[7741440]{0:T(1024)(128)(4,1)}), s8[3547136]{0:T(1024)(128)(4,1)S(1)}, s32[]{:S(2)}) async-start(s8[7741440]{0:T(1024)(128)(4,1)} %bitcast.80), calls=%async_computation.2 | async-start | bytes 7094272
  74.8 2.7 %slice-start.1 = ((s8[7741440]{0:T(1024)(128)(4,1)}), s8[4194304]{0:T(1024)(128)(4,1)S(1)}, s32[]{:S(2)}) async-start(s8[7741440]{0:T(1024)(128)(4,1)} %bitcast.80), calls=%async_computation.3 | async-start | bytes 8388608
  84.3 19.5 %all-to-all-start = ((bf16[8,2,3955]{2,1,0:T(2,128)(2,1)}), bf16[8,2,3955]{2,1,0:T(2,128)(2,1)S(1)}, u32[]{:S(2)}, u32[]{:S(2)}) async-start(bf16[8,2,3955]{2,1,0:T(2,128)(2,1)} %reshape.72), calls=%async_computation | async-start | bytes 253952 | tf_op jit(solution)/shard_map/all_to_all | solution.py:531
  105.6 10.6 %all-to-all-start.1 = ((bf16[8,2,3955]{2,1,0:T(2,128)(2,1)}), bf16[8,2,3955]{2,1,0:T(2,128)(2,1)S(1)}, u32[]{:S(2)}, u32[]{:S(2)}) async-start(bf16[8,2,3955]{2,1,0:T(2,128)(2,1)} %reshape.74), calls=%async_computation.1 | async-start | bytes 253952 | tf_op jit(solution)/shard_map/all_to_all | solution.py:536

commit v3 on v2

--- a/solution.py
+++ b/solution.py
@@ -312,9 +312,10 @@
                 landed(part, shard, "core_own").wait_recv()
                 landed(part, shard, "core_y").wait_recv()
 
-    for tick in range(2 * count + depth):
+    begins = (0, 1, 3)
+    for tick in range(begins[-1] + depth + 2):
         for part in range(count):
-            d = tick - 2 * part
+            d = tick - begins[part]
             if 0 <= d < depth:
                 stage(part, d)
             elif d == depth:
@@ -378,7 +379,7 @@
             jax.ShapeDtypeStruct(whole[2], jnp.bfloat16),
         ],
         in_specs=[pl.BlockSpec(memory_space=pltpu.VMEM)]
-        + [pl.BlockSpec(memory_space=pl.ANY)] * count,
+        + [pl.BlockSpec(memory_space=pltpu.HBM)] * count,
         out_specs=[
             pl.BlockSpec(memory_space=pltpu.VMEM),
             pl.BlockSpec(memory_space=pl.ANY),
@@ -405,6 +406,128 @@
     )(latent, *parts)
 
 
+def mix_kernel(
+    wide, size, query, key, value, mixed,
+    states, came, prefix, back, local, out_sem, in_sem,
+):
+    w = lax.axis_index("wide")
+    heads, tokens, lanes = query.shape
+    piece = states.shape[1]
+    barrier = pltpu.get_barrier_semaphore()
+
+    def peer(step):
+        return lax.rem(w + step, wide)
+
+    for step in range(1, wide):
+        pl.semaphore_signal(
+            barrier, inc=1, device_id={"wide": peer(step)}, device_id_type=MESH
+        )
+
+    for head in range(heads):
+        outer = lax.dot_general(
+            key[head], value[head], (((0,), (0,)), ((), ())), preferred_element_type=jnp.float32
+        ).astype(jnp.bfloat16)
+        for row in range(0, lanes, 16):
+            index, at = divmod(head * lanes + row, piece)
+            states[index, at : at + 16] = outer[row : row + 16]
+
+    def push(phase, step):
+        to = peer(step)
+        source, target = ((states, came), (prefix, back))[phase]
+        return pltpu.make_async_remote_copy(
+            src_ref=source.at[to],
+            dst_ref=target.at[w],
+            send_sem=out_sem.at[phase, step],
+            recv_sem=in_sem.at[phase, step],
+            device_id={"wide": to},
+            device_id_type=MESH,
+        )
+
+    def arrived(phase, step):
+        sender = lax.rem(w + wide - step, wide)
+        target = (came, back)[phase]
+        return pltpu.make_async_remote_copy(
+            src_ref=target.at[sender],
+            dst_ref=target.at[sender],
+            send_sem=out_sem.at[phase, step],
+            recv_sem=in_sem.at[phase, step],
+            device_id={"wide": sender},
+            device_id_type=MESH,
+        )
+
+    row_ids = lax.broadcasted_iota(jnp.int32, (tokens, tokens), 0)
+    col_ids = lax.broadcasted_iota(jnp.int32, (tokens, tokens), 1)
+    spot = lax.broadcasted_iota(jnp.int32, (tokens, lanes), 1)
+
+    def inside_frame(head):
+        scores = lax.dot_general(
+            query[head], key[head], (((1,), (1,)), ((), ())), preferred_element_type=jnp.float32
+        )
+        scores = jnp.where(col_ids <= row_ids, scores, 0.0)
+        below = jnp.sum(scores, axis=1, keepdims=True)
+        above = jnp.dot(
+            scores.astype(jnp.bfloat16), value[head], preferred_element_type=jnp.float32
+        )
+        local[head] = jnp.where(spot == size, below, above)
+
+    pl.semaphore_wait(barrier, wide - 1)
+    for step in range(1, wide):
+        push(0, step).start()
+    came[w] = states[w]
+    for head in range(heads // 2):
+        inside_frame(head)
+    for step in range(1, wide):
+        arrived(0, step).wait_recv()
+    running = jnp.zeros(states.shape[1:], jnp.float32)
+    for frame in range(wide):
+        prefix[frame] = running.astype(jnp.bfloat16)
+        running = running + came[frame].astype(jnp.float32)
+    for step in range(1, wide):
+        push(1, step).start()
+    back[w] = prefix[w]
+    for head in range(heads // 2, heads):
+        inside_frame(head)
+    for step in range(1, wide):
+        arrived(1, step).wait_recv()
+    for head in range(heads):
+        parts = []
+        for row in range(0, lanes, 16):
+            index, at = divmod(head * lanes + row, piece)
+            parts.append(back[index, at : at + 16])
+        carried = jnp.dot(
+            query[head], jnp.concatenate(parts, axis=0), preferred_element_type=jnp.float32
+        )
+        whole = local[head] + carried
+        mixed[head] = (whole / whole[:, size : size + 1]).astype(jnp.bfloat16)
+    for phase in range(2):
+        for step in range(1, wide):
+            push(phase, step).wait_send()
+
+
+def mix_frames(query, key, value, size):
+    wide = lax.axis_size("wide")
+    heads, tokens, lanes = query.shape
+    pieces = (wide, heads * lanes // wide, lanes)
+    return pl.pallas_call(
+        functools.partial(mix_kernel, wide, size),
+        out_shape=jax.ShapeDtypeStruct(query.shape, jnp.bfloat16),
+        in_specs=[pl.BlockSpec(memory_space=pltpu.VMEM)] * 3,
+        out_specs=pl.BlockSpec(memory_space=pltpu.VMEM),
+        scratch_shapes=[
+            pltpu.VMEM(pieces, jnp.bfloat16),
+            pltpu.VMEM(pieces, jnp.bfloat16),
+            pltpu.VMEM(pieces, jnp.bfloat16),
+            pltpu.VMEM(pieces, jnp.bfloat16),
+            pltpu.VMEM(query.shape, jnp.float32),
+            pltpu.SemaphoreType.DMA((2, wide)),
+            pltpu.SemaphoreType.DMA((2, wide)),
+        ],
+        compiler_params=pltpu.CompilerParams(
+            collective_id=1, has_side_effects=True, vmem_limit_bytes=32 * 1024 * 1024
+        ),
+    )(query, key, value)
+
+
 def shifted(x, axis, by):
     size = lax.axis_size(axis)
     pairs = [(i, i + by) for i in range(size) if 0 <= i + by < size]
@@ -503,6 +626,15 @@
         (jax.nn.elu(key_raw) + 1.0).astype(jnp.bfloat16).reshape(token_count, heads_here, HEAD_DIM)
     )
     val_heads = val_rows.reshape(token_count, heads_here, HEAD_DIM)
+    if wide * 16 <= heads_here * LANE and heads_here * LANE % (wide * 16) == 0:
+
+        def padded(rows):
+            return jnp.pad(rows, ((0, 0), (0, 0), (0, LANE - HEAD_DIM))).transpose(1, 0, 2)
+
+        place = lax.broadcasted_iota(jnp.int32, (heads_here, token_count, LANE), 2)
+        value = jnp.where(place == HEAD_DIM, jnp.bfloat16(1), padded(val_heads))
+        mixed = mix_frames(padded(query_feat), padded(key_feat), value, HEAD_DIM)
+        return mixed.transpose(1, 0, 2)[:, :, :HEAD_DIM].reshape(token_count, -1)
     scores = jnp.einsum("thd,shd->hts", query_feat, key_feat, preferred_element_type=jnp.float32)
     row_ids = lax.broadcasted_iota(jnp.int32, (token_count, token_count), 0)
     col_ids = lax.broadcasted_iota(jnp.int32, (token_count, token_count), 1)

time: 120 us -> 112 us (0.933)
  Pallas kernels: 70.8 us -> 91.3 us
  starting transfers between devices: 15.5 us -> 0 us
  waiting for transfers between devices: 10.5 us -> 0 us
  other arithmetic: 2.7 us -> 0.26 us
  local copies, waits for them, and re-layouts: 7.61 us -> 5.91 us
  matrix products: 12.4 us -> 13.8 us
    pallas_call x0 -> x1, Pallas kernels: none -> 18.2 us  [mix_frames(): pl.pallas_call(functools.partial(mix_kernel, wide, size), out_shape=jax.S...]
    all_to_all x2 -> x0, starting transfers between devices: 15.5 us -> none  [the longest x1 12.1 us: per_device(): lax.all_to_all(piece_grid.astype(jnp.bfloat16), 'wide', split_axis=0, con...]
    all_to_all x2 -> x0, waiting for transfers between devices: 10.5 us -> none  [the longest x1 6.57 us: per_device(): lax.all_to_all(partial_sums.astype(jnp.bfloat16), 'wide', split_axis=0, c...]
    dot_general x6 -> x0, matrix products: 2.9 us -> none  [the longest x1 1.26 us: per_device(): jnp.einsum('hts,she->the', scores.astype(jnp.bfloat16), val_heads, prefer...]
    pallas_call x1, Pallas kernels: 70.8 us -> 73.1 us  [conv_block(): pl.pallas_call(functools.partial(block_kernel, wide, narrow, shapes), out...]
    dot_general x1, matrix products: 1.86 us -> 4.06 us  [per_device(): jnp.dot(embedded, qkv_weight[1], preferred_element_type=jnp.float32)]
    unnamed x16 -> x10, local copies, waits for them, and re-layouts: 5.95 us -> 4.01 us
    dot_general x1, matrix products: 1.51 us -> 3.22 us  [per_device(): jnp.dot(embedded, qkv_weight[2], preferred_element_type=jnp.float32)]
  transfers between devices with their start and end apart: 2 -> 0, of which waited for: 2 -> 0; matrix products, arithmetic and copies ran while one was open for 3% -> 0% of each run, Pallas kernels for 0% -> 0%
where the time goes in v3:
time: 112 us; the launch traced here: 111 us
  Pallas kernels  91.3 us (82%)
  matrix products  13.8 us (12%)
  local copies, waits for them, and re-layouts  5.91 us (5%)
    pallas_call x1, Pallas kernels, conv_block(): pl.pallas_call(functools.partial(block_kernel, wide, narrow, shapes), out...  73.1 us
    pallas_call x1, Pallas kernels, mix_frames(): pl.pallas_call(functools.partial(mix_kernel, wide, size), out_shape=jax.S...  18.2 us
    dot_general x1, matrix products, per_device(): jnp.dot(embedded, qkv_weight[1], preferred_element_type=jnp.float32)  4.06 us
    unnamed x10, local copies, waits for them, and re-layouts  4.01 us
    dot_general x1, matrix products, per_device(): jnp.dot(embedded, qkv_weight[0], preferred_element_type=jnp.float32)  3.94 us
    dot_general x1, matrix products, per_device(): jnp.dot(embedded, qkv_weight[2], preferred_element_type=jnp.float32)  3.22 us
    dot_general x1, matrix products, embedded_fused(): lax.dot_general(patches.reshape(-1, patches.shape[2]), weights.reshape(-1...  2.58 us

profile of v3, /device:TPU:0, one launch (start us, length us, event | category | flops | bytes accessed | tf_op | source)
XLA Modules:
  0.0 111.4 jit_solution(15293943965250908441)
XLA Ops:
  0.0 0.0 copy-start
  0.0 1.1 copy-done
  1.1 0.0 copy-start.1
  1.1 1.0 copy-done.1
  2.1 0.0 copy-start.2
  2.1 1.0 copy-done.2
  3.1 0.0 copy-start.3
  3.1 0.9 copy-done.3
  4.0 73.1 %shard_map.55 = (bf16[4,96,1024]{2,1,0:T(8,128)(2,1)S(1)}, bf16[8,280,1024]{2,1,0:T(8,128)(2,1)S(1)}) custom-call(bf16[1,8,48,256]{3,2,1,0:T(8,128)(2,1)S(1)} %copy-done.3, bf16[32,6912]{1,0:T(8,128)(2,1)S(1)} %bitcast.47, bf16[32,6912]{1,0:T(8,128)(2,1)S(1)} %bitcast.48, bf16[280,1024]{1,0:T(8,128)(2,1)S(1)} %bitcast.46), custom_call_target="tpu_custom_call" | custom-call | tf_op jit(solution)/shard_map/pallas_call | solution.py:375
  77.1 2.6 %convolution_convert_fusion = bf16[384,2240]{0,1:T(8,128)(2,1)S(1)} fusion(bf16[384,1024]{1,0:T(8,128)(2,1)S(1)} %bitcast.50, bf16[2240,1024]{1,0:T(8,128)(2,1)S(1)} %bitcast.49), kind=kOutput, calls=%fused_computation | convolution fusion | flops 1762467840 | bytes 7094272 | tf_op jit(solution)/shard_map/dot_general | solution.py:600
  79.7 0.0 copy-start.4
  79.7 4.1 %fusion.27 = bf16[384,560]{0,1:T(8,128)(2,1)S(1)} fusion(bf16[384,2240]{0,1:T(8,128)(2,1)S(1)} %convolution_convert_fusion, bf16[3,2240,560]{1,2,0:T(8,128)(2,1)} %param.9), kind=kOutput, calls=%fused_computation.20 | convolution fusion | flops 964454400 | bytes 4730880 | tf_op jit(solution)/shard_map/dot_general | solution.py:616
  83.8 0.3 copy.7
  84.1 0.0 copy-done.4
  84.1 3.2 %fusion.9 = bf16[384,560]{0,1:T(8,128)(2,1)S(1)} fusion(bf16[384,2240]{0,1:T(8,128)(2,1)S(1)} %convolution_convert_fusion, bf16[3,2240,560]{1,2,0:T(8,128)(2,1)} %param.9), kind=kOutput, calls=%fused_computation.14 | convolution fusion | flops 963594240 | bytes 4730880 | tf_op jit(solution)/shard_map/dot_general | solution.py:617
  87.3 0.3 copy.8
  87.6 0.3 select_bitcast_fusion
  87.9 3.9 %fusion.18 = bf16[384,560]{0,1:T(8,128)(2,1)S(1)} fusion(bf16[384,2240]{0,1:T(8,128)(2,1)} %copy-done.4, bf16[3,2240,560]{1,2,0:T(8,128)(2,1)} %param.9), kind=kOutput, calls=%fused_computation.17 | convolution fusion | flops 964454400 | bytes 4730880 | tf_op jit(solution)/shard_map/dot_general | solution.py:615
  91.8 0.3 copy.6
  92.1 0.1 pad_bitcast_fusion.1.query
  92.2 18.2 %shard_map.56 = bf16[5,384,128]{2,1,0:T(8,128)(2,1)S(1)} custom-call(bf16[5,384,128]{2,1,0:T(8,128)(2,1)S(1)} %pad_bitcast_fusion.1.query, bf16[5,384,128]{2,1,0:T(8,128)(2,1)S(1)} %get-tuple-element.10.key, bf16[5,384,128]{2,1,0:T(8,128)(2,1)S(1)} %get-tuple-element.9.value), custom_call_target="tpu_custom_call" | custom-call | tf_op jit(solution)/shard_map/pallas_call | solution.py:511
  110.4 1.0 copy.9
  (1 shorter events, 0.0 us)
Async XLA Ops:
  0.0 1.1 copy-start
  1.1 1.0 copy-start.1
  2.1 1.0 copy-start.2
  3.1 0.9 copy-start.3
  79.7 4.4 %copy-start.4 = (bf16[384,2240]{0,1:T(8,128)(2,1)}, bf16[384,2240]{0,1:T(8,128)(2,1)S(1)}, u32[]{:S(2)}) copy-start(bf16[384,2240]{0,1:T(8,128)(2,1)S(1)} %convolution_convert_fusion) | copy-start | bytes 5160964

commit v4 on v3

--- a/solution.py
+++ b/solution.py
@@ -14,7 +14,7 @@
 
 def strips(lanes):
     half = lanes // LANE // 2
-    return half, max(1, half // 3)
+    return half, max(1, half * 41 // 100)
 
 
 def block_kernel(
@@ -312,7 +312,7 @@
                 landed(part, shard, "core_own").wait_recv()
                 landed(part, shard, "core_y").wait_recv()
 
-    begins = (0, 1, 3)
+    begins = (0, 2, 4)
     for tick in range(begins[-1] + depth + 2):
         for part in range(count):
             d = tick - begins[part]
@@ -407,12 +407,21 @@
 
 
 def mix_kernel(
-    wide, size, query, key, value, mixed,
+    wide, size, joint, mixed,
     states, came, prefix, back, local, out_sem, in_sem,
 ):
     w = lax.axis_index("wide")
-    heads, tokens, lanes = query.shape
+    heads, lanes, tokens = local.shape
     piece = states.shape[1]
+    spare = lanes - size
+    blank = jnp.zeros((spare, tokens), jnp.bfloat16)
+    mark = lax.broadcasted_iota(jnp.int32, (spare, tokens), 0) == 0
+    ones = jnp.where(mark, 1.0, 0.0).astype(jnp.bfloat16)
+
+    def block(which, head, tail):
+        at = (which * heads + head) * size
+        return jnp.concatenate([joint[at : at + size], tail], axis=0)
+
     barrier = pltpu.get_barrier_semaphore()
 
     def peer(step):
@@ -425,7 +434,8 @@
 
     for head in range(heads):
         outer = lax.dot_general(
-            key[head], value[head], (((0,), (0,)), ((), ())), preferred_element_type=jnp.float32
+            block(2, head, ones), block(1, head, blank), (((1,), (1,)), ((), ())),
+            preferred_element_type=jnp.float32,
         ).astype(jnp.bfloat16)
         for row in range(0, lanes, 16):
             index, at = divmod(head * lanes + row, piece)
@@ -457,16 +467,17 @@
 
     row_ids = lax.broadcasted_iota(jnp.int32, (tokens, tokens), 0)
     col_ids = lax.broadcasted_iota(jnp.int32, (tokens, tokens), 1)
-    spot = lax.broadcasted_iota(jnp.int32, (tokens, lanes), 1)
+    spot = lax.broadcasted_iota(jnp.int32, (lanes, tokens), 0)
 
     def inside_frame(head):
         scores = lax.dot_general(
-            query[head], key[head], (((1,), (1,)), ((), ())), preferred_element_type=jnp.float32
-        )
-        scores = jnp.where(col_ids <= row_ids, scores, 0.0)
-        below = jnp.sum(scores, axis=1, keepdims=True)
+            block(1, head, blank), block(0, head, blank), (((0,), (0,)), ((), ())),
+            preferred_element_type=jnp.float32,
+        )
+        scores = jnp.where(row_ids <= col_ids, scores, 0.0)
+        below = jnp.sum(scores, axis=0, keepdims=True)
         above = jnp.dot(
-            scores.astype(jnp.bfloat16), value[head], preferred_element_type=jnp.float32
+            block(2, head, blank), scores.astype(jnp.bfloat16), preferred_element_type=jnp.float32
         )
         local[head] = jnp.where(spot == size, below, above)
 
@@ -495,37 +506,40 @@
             index, at = divmod(head * lanes + row, piece)
             parts.append(back[index, at : at + 16])
         carried = jnp.dot(
-            query[head], jnp.concatenate(parts, axis=0), preferred_element_type=jnp.float32
+            jnp.concatenate(parts, axis=0), block(0, head, blank),
+            preferred_element_type=jnp.float32,
         )
         whole = local[head] + carried
-        mixed[head] = (whole / whole[:, size : size + 1]).astype(jnp.bfloat16)
+        mixed[head * size : (head + 1) * size] = (
+            whole[:size] / whole[size : size + 1]
+        ).astype(jnp.bfloat16)
     for phase in range(2):
         for step in range(1, wide):
             push(phase, step).wait_send()
 
 
-def mix_frames(query, key, value, size):
+def mix_frames(joint, size):
     wide = lax.axis_size("wide")
-    heads, tokens, lanes = query.shape
-    pieces = (wide, heads * lanes // wide, lanes)
+    heads, tokens = joint.shape[0] // 3 // size, joint.shape[1]
+    pieces = (wide, heads * LANE // wide, LANE)
     return pl.pallas_call(
         functools.partial(mix_kernel, wide, size),
-        out_shape=jax.ShapeDtypeStruct(query.shape, jnp.bfloat16),
-        in_specs=[pl.BlockSpec(memory_space=pltpu.VMEM)] * 3,
+        out_shape=jax.ShapeDtypeStruct((heads * size, tokens), jnp.bfloat16),
+        in_specs=[pl.BlockSpec(memory_space=pltpu.VMEM)],
         out_specs=pl.BlockSpec(memory_space=pltpu.VMEM),
         scratch_shapes=[
             pltpu.VMEM(pieces, jnp.bfloat16),
             pltpu.VMEM(pieces, jnp.bfloat16),
             pltpu.VMEM(pieces, jnp.bfloat16),
             pltpu.VMEM(pieces, jnp.bfloat16),
-            pltpu.VMEM(query.shape, jnp.float32),
+            pltpu.VMEM((heads, LANE, tokens), jnp.float32),
             pltpu.SemaphoreType.DMA((2, wide)),
             pltpu.SemaphoreType.DMA((2, wide)),
         ],
         compiler_params=pltpu.CompilerParams(
             collective_id=1, has_side_effects=True, vmem_limit_bytes=32 * 1024 * 1024
         ),
-    )(query, key, value)
+    )(joint)
 
 
 def shifted(x, axis, by):
@@ -612,6 +626,17 @@
     embedded = embed(latent, conv_first, conv_second, embed_weight)
     heads_here = qkv_weight.shape[2] // HEAD_DIM
     token_count = embedded.shape[0]
+    if heads_here * LANE % (wide * 16) == 0:
+        turned = qkv_weight.transpose(0, 2, 1).reshape(-1, qkv_weight.shape[1])
+        joint = lax.dot_general(
+            turned,
+            lax.optimization_barrier(embedded),
+            (((1,), (1,)), ((), ())),
+            preferred_element_type=jnp.float32,
+        )
+        row = lax.broadcasted_iota(jnp.int32, joint.shape, 0)
+        joint = jnp.where(row < 2 * qkv_weight.shape[2], jax.nn.elu(joint) + 1.0, joint)
+        return mix_frames(joint.astype(jnp.bfloat16), HEAD_DIM).T
     query_raw = jnp.dot(embedded, qkv_weight[0], preferred_element_type=jnp.float32)
     key_raw = jnp.dot(embedded, qkv_weight[1], preferred_element_type=jnp.float32)
     val_rows = jnp.dot(embedded, qkv_weight[2], preferred_element_type=jnp.float32).astype(
@@ -626,15 +651,6 @@
         (jax.nn.elu(key_raw) + 1.0).astype(jnp.bfloat16).reshape(token_count, heads_here, HEAD_DIM)
     )
     val_heads = val_rows.reshape(token_count, heads_here, HEAD_DIM)
-    if wide * 16 <= heads_here * LANE and heads_here * LANE % (wide * 16) == 0:
-
-        def padded(rows):
-            return jnp.pad(rows, ((0, 0), (0, 0), (0, LANE - HEAD_DIM))).transpose(1, 0, 2)
-
-        place = lax.broadcasted_iota(jnp.int32, (heads_here, token_count, LANE), 2)
-        value = jnp.where(place == HEAD_DIM, jnp.bfloat16(1), padded(val_heads))
-        mixed = mix_frames(padded(query_feat), padded(key_feat), value, HEAD_DIM)
-        return mixed.transpose(1, 0, 2)[:, :, :HEAD_DIM].reshape(token_count, -1)
     scores = jnp.einsum("thd,shd->hts", query_feat, key_feat, preferred_element_type=jnp.float32)
     row_ids = lax.broadcasted_iota(jnp.int32, (token_count, token_count), 0)
     col_ids = lax.broadcasted_iota(jnp.int32, (token_count, token_count), 1)

time: 112 us -> 104 us (0.929)
  matrix products: 13.8 us -> 7.21 us
    dot_general x3 -> x1, matrix products: 11.2 us -> 5.18 us  [per_device(): lax.dot_general(turned, lax.optimization_barrier(embedded), (((1,), (1,))...]
    pallas_call x1, Pallas kernels: 73.1 us -> 69.9 us  [conv_block(): pl.pallas_call(functools.partial(block_kernel, wide, narrow, shapes), out...]
    pallas_call x1, Pallas kernels: 18.2 us -> 21 us  [mix_frames(): pl.pallas_call(functools.partial(mix_kernel, wide, size), out_shape=jax.S...]
    unnamed x10 -> x11, local copies, waits for them, and re-layouts: 4.01 us -> 5.91 us
where the time goes in v4:
time: 104 us
  Pallas kernels  90.9 us (87%)
  matrix products  7.21 us (7%)
  local copies, waits for them, and re-layouts  5.91 us (6%)
    pallas_call x1, Pallas kernels, conv_block(): pl.pallas_call(functools.partial(block_kernel, wide, narrow, shapes), out...  69.9 us
    pallas_call x1, Pallas kernels, mix_frames(): pl.pallas_call(functools.partial(mix_kernel, wide, size), out_shape=jax.S...  21 us
    unnamed x11, local copies, waits for them, and re-layouts  5.91 us
    dot_general x1, matrix products, per_device(): lax.dot_general(turned, lax.optimization_barrier(embedded), (((1,), (1,))...  5.18 us

profile of v4, /device:TPU:0, one launch (start us, length us, event | category | flops | bytes accessed | tf_op | source)
XLA Modules:
  0.0 104.1 jit_solution(9863703670878941186)
XLA Ops:
  0.0 0.0 copy-start
  0.0 1.1 %copy-done = bf16[1024,280]{0,1:T(8,128)(2,1)S(1)} copy-done((bf16[1024,280]{0,1:T(8,128)(2,1)S(1)}, bf16[1024,280]{0,1:T(8,128)(2,1)}, u32[]{:S(2)}) %copy-start) | copy-done | bytes 573464
  1.1 0.0 copy-start.1
  1.1 1.0 copy-done.1
  2.1 0.0 copy-start.2
  2.1 1.0 copy-done.2
  3.1 0.0 copy-start.3
  3.1 0.9 copy-done.3
  4.0 69.9 %shard_map.55 = (bf16[4,96,1024]{2,1,0:T(8,128)(2,1)S(1)}, bf16[8,280,1024]{2,1,0:T(8,128)(2,1)S(1)}) custom-call(bf16[1,8,48,256]{3,2,1,0:T(8,128)(2,1)S(1)} %copy-done.3, bf16[32,6912]{1,0:T(8,128)(2,1)S(1)} %bitcast.21, bf16[32,6912]{1,0:T(8,128)(2,1)S(1)} %bitcast.22, bf16[280,1024]{1,0:T(8,128)(2,1)S(1)} %bitcast.20), custom_call_target="tpu_custom_call" | custom-call | tf_op jit(solution)/shard_map/pallas_call | solution.py:375
  73.9 0.0 copy-start.4
  73.9 2.0 %convolution_convert_fusion = bf16[384,2240]{1,0:T(8,128)(2,1)S(1)} fusion(bf16[384,1024]{1,0:T(8,128)(2,1)S(1)} %bitcast.24, bf16[2240,1024]{1,0:T(8,128)(2,1)S(1)} %bitcast.23), kind=kOutput, calls=%fused_computation.2 | convolution fusion | flops 1762467840 | bytes 7094272 | tf_op jit(solution)/shard_map/dot_general | solution.py:614
  76.0 1.1 %copy-done.4 = bf16[3,2240,560]{1,2,0:T(8,128)(2,1)S(1)} copy-done((bf16[3,2240,560]{1,2,0:T(8,128)(2,1)S(1)}, bf16[3,2240,560]{1,2,0:T(8,128)(2,1)}, u32[]{:S(2)}) %copy-start.4) | copy-done | bytes 7526424
  77.1 5.2 %fusion.3.joint = bf16[1680,384]{1,0:T(8,128)(2,1)S(1)} fusion(bf16[384,2240]{1,0:T(8,128)(2,1)S(1)} %convolution_convert_fusion, bf16[1680,2240]{1,0:T(8,128)(2,1)S(1)} %bitcast.25, pred[1680]{0:T(1024)(128)(4,1)S(1)} %iota_compare_fusion), kind=kOutput, calls=%fused_computation.7 | convolution fusion | flops 2894008320 | bytes 10538640 | tf_op jit(solution)/shard_map/dot_general | solution.py:631
  82.3 21.0 %shard_map.56 = bf16[560,384]{1,0:T(8,128)(2,1)S(1)} custom-call(bf16[1680,384]{1,0:T(8,128)(2,1)S(1)} %fusion.3.joint), custom_call_target="tpu_custom_call" | custom-call | tf_op jit(solution)/shard_map/pallas_call | solution.py:525
  103.3 0.8 copy.7
  (1 shorter events, 0.0 us)
Async XLA Ops:
  0.0 1.1 %copy-start = (bf16[1024,280]{0,1:T(8,128)(2,1)S(1)}, bf16[1024,280]{0,1:T(8,128)(2,1)}, u32[]{:S(2)}) copy-start(bf16[1024,280]{0,1:T(8,128)(2,1)} %param.8) | copy-start | bytes 1720324
  1.1 1.0 copy-start.1
  2.1 1.0 copy-start.2
  3.1 0.9 copy-start.3
  73.9 3.2 %copy-start.4 = (bf16[3,2240,560]{1,2,0:T(8,128)(2,1)S(1)}, bf16[3,2240,560]{1,2,0:T(8,128)(2,1)}, u32[]{:S(2)}) copy-start(bf16[3,2240,560]{1,2,0:T(8,128)(2,1)} %param.9) | copy-start | bytes 22579204

commit v5 on v4

--- a/solution.py
+++ b/solution.py
@@ -401,7 +401,7 @@
             pltpu.SemaphoreType.DMA((3,)),
         ],
         compiler_params=pltpu.CompilerParams(
-            collective_id=0, has_side_effects=True, vmem_limit_bytes=40 * 1024 * 1024
+            collective_id=0, has_side_effects=True, vmem_limit_bytes=56 * 1024 * 1024
         ),
     )(latent, *parts)
 

time: 104 us -> 106 us (1.019)
  local copies, waits for them, and re-layouts: 5.91 us -> 0.8 us
  Pallas kernels: 90.9 us -> 94.7 us
  matrix products: 7.21 us -> 9.9 us
    unnamed x11 -> x3, local copies, waits for them, and re-layouts: 5.91 us -> 0.8 us
    pallas_call x1, Pallas kernels: 69.9 us -> 73.9 us  [conv_block(): pl.pallas_call(functools.partial(block_kernel, wide, narrow, shapes), out...]
    dot_general x1, matrix products: 2.03 us -> 4.72 us  [embedded_fused(): lax.dot_general(patches.reshape(-1, patches.shape[2]), weights.reshape(-1...]
where the time goes in v5:
time: 106 us; the launch traced here: 105 us
  Pallas kernels  94.7 us (89%)
  matrix products  9.9 us (9%)
    pallas_call x1, Pallas kernels, conv_block(): pl.pallas_call(functools.partial(block_kernel, wide, narrow, shapes), out...  73.9 us
    pallas_call x1, Pallas kernels, mix_frames(): pl.pallas_call(functools.partial(mix_kernel, wide, size), out_shape=jax.S...  20.7 us
    dot_general x1, matrix products, per_device(): lax.dot_general(turned, lax.optimization_barrier(embedded), (((1,), (1,))...  5.18 us
    dot_general x1, matrix products, embedded_fused(): lax.dot_general(patches.reshape(-1, patches.shape[2]), weights.reshape(-1...  4.72 us

profile of v5, /device:TPU:0, one launch (start us, length us, event | category | flops | bytes accessed | tf_op | source)
XLA Modules:
  0.0 105.4 jit_solution(4107112434644939809)
XLA Ops:
  0.0 73.9 %shard_map.55 = (bf16[4,96,1024]{2,1,0:T(8,128)(2,1)}, bf16[8,280,1024]{2,1,0:T(8,128)(2,1)}) custom-call(bf16[1,8,48,256]{3,2,1,0:T(8,128)(2,1)} %latent.1, bf16[32,6912]{1,0:T(8,128)(2,1)} %bitcast.21, bf16[32,6912]{1,0:T(8,128)(2,1)} %bitcast.22, bf16[280,1024]{1,0:T(8,128)(2,1)} %bitcast.20), custom_call_target="tpu_custom_call" | custom-call | tf_op jit(solution)/shard_map/pallas_call | solution.py:375
  73.9 0.0 copy-start
  73.9 4.7 %convolution_convert_fusion = bf16[384,2240]{1,0:T(8,128)(2,1)S(1)} fusion(bf16[384,1024]{1,0:T(8,128)(2,1)} %bitcast.25, bf16[2240,1024]{1,0:T(8,128)(2,1)} %bitcast.24), kind=kOutput, calls=%fused_computation.2 | convolution fusion | flops 1762467840 | bytes 7094272 | tf_op jit(solution)/shard_map/dot_general | solution.py:614
  78.7 0.0 copy-done
  78.7 5.2 %fusion.3.joint = bf16[1680,384]{1,0:T(8,128)(2,1)S(1)} fusion(bf16[384,2240]{1,0:T(8,128)(2,1)S(1)} %convolution_convert_fusion, bf16[1680,2240]{1,0:T(8,128)(2,1)S(1)} %bitcast.23, pred[1680]{0:T(1024)(128)(4,1)S(1)} %iota_compare_fusion), kind=kOutput, calls=%fused_computation.7 | convolution fusion | flops 2894008320 | bytes 10538640 | tf_op jit(solution)/shard_map/dot_general | solution.py:631
  83.9 20.7 %shard_map.56 = bf16[560,384]{1,0:T(8,128)(2,1)S(1)} custom-call(bf16[1680,384]{1,0:T(8,128)(2,1)S(1)} %fusion.3.joint), custom_call_target="tpu_custom_call" | custom-call | tf_op jit(solution)/shard_map/pallas_call | solution.py:525
  104.7 0.8 copy.7
  (1 shorter events, 0.0 us)
Async XLA Ops:
  73.9 4.8 %copy-start = (bf16[3,2240,560]{1,2,0:T(8,128)(2,1)S(1)}, bf16[3,2240,560]{1,2,0:T(8,128)(2,1)}, u32[]{:S(2)}) copy-start(bf16[3,2240,560]{1,2,0:T(8,128)(2,1)} %param.9) | copy-start | bytes 22579204
